TPU v7x, 512 devices: a whole 4x8x8 slice. The times are simulated.
512 devices in a mesh: ty: 16 (over z, core), tx: 32 (over x, y).
Axes of the slice: x: 4, y: 8, z: 8, core: 2. Of those that a mesh axis runs over, the one named last changes fastest.
Arguments:
- points: float32 [16, 32, 3, 4096], P('ty', 'tx'), may hold values from 0 to 64
- probes: float32 [16, 32, 8, 4096], P('ty', 'tx'), may hold values from -0.6 to 0.6
- near_boxes: int32 [16, 32, 16, 27], P('ty', 'tx'), may hold values from -1 to 8191, as said below
- leaf_bases: float32 [16, 32, 64, 4096], P('ty', 'tx'), may hold values from -0.375 to 0.375
- box_transfer: float32 [16, 32, 16, 64, 64], P('ty', 'tx'), may hold values from -1 to 1
- upper_transfer: float32 [9, 2, 64, 64], replicated, may hold values from -1 to 1
Outputs:
- near_field: float32 [16, 32, 8, 4096], P('ty', 'tx')
- leaf_factor: float32 [16, 32, 16, 64, 64], P('ty', 'tx')
- ancestors: float32 [16, 32, 10, 64, 64], P('ty', 'tx')
Inputs may be any that keep to these rules, and one draw needn't show every extreme that they name: `near_boxes`: box k of tile (ty, tx) sits at grid cell (2 ty + k % 2, 2 tx + (k // 2) % 2, k // 4). Slot s of a box's list names the box at cell offset (s // 9 - 1, (s // 3) % 3 - 1, s % 3 - 1) from it, or -1; slot 13 names the box itself. Every named box lies in the box's own tile or one of the eight tiles around it.
All inputs are finite; a program needn't handle non-finite values.
Results may differ from a plain program's by a relative error of at most 0.004.
Values sent between devices are 32-bit elements; how exact they have to be, the bound alone decides.
A program may use at most 64 MiB of HBM per device.

v0:
```python
import jax
import jax.numpy as jnp
from jax import lax
from jax.sharding import PartitionSpec as P

BOX_PTS = 256


length_scale = 1.0
root_three = 1.7320508075688772


def with_halo(shard, sides, width):
    for axis, dim in sides:
        peers, length = (lax.axis_size(axis), shard.shape[dim])
        up = [(i, (i + 1) % peers) for i in range(peers - 1)]
        down = [(j, i) for i, j in up]
        last = lax.slice_in_dim(shard, length - width, length, axis=dim)
        first = lax.slice_in_dim(shard, 0, width, axis=dim)
        before = lax.ppermute(last, axis, up)
        after = lax.ppermute(first, axis, down)
        shard = jnp.concatenate([before, shard, after], axis=dim)
    return shard


def from_partner(value, axis, bit):
    mask = 2**bit
    pairs = [(source, source ^ mask) for source in range(lax.axis_size(axis))]
    return lax.ppermute(value, axis, pairs)


def kernel_block(target, source):
    dist_sq = jnp.zeros((source.shape[0], target.shape[1], source.shape[2]), jnp.float32)
    for coord in range(3):
        delta = target[coord][None, :, None] - source[:, coord][:, None, :]
        dist_sq = dist_sq + delta * delta
    scaled = root_three * jnp.sqrt(dist_sq) / length_scale
    return ((1.0 + scaled) * jnp.exp(-scaled)).astype(jnp.bfloat16)


def upper_factor(gram_sum):
    return jnp.swapaxes(jnp.linalg.cholesky(gram_sum), -1, -2)


def gram_of(term):
    return jnp.matmul(jnp.swapaxes(term, -1, -2), term, precision=lax.Precision.HIGHEST)


def on_device(points, probes, near_boxes, leaf_bases, box_transfer, upper_transfer):
    row_width = points.shape[3]
    boxes_dev = row_width // BOX_PTS
    joined = jnp.concatenate([points, probes], axis=2)
    channels = joined.shape[2]
    extended = with_halo(joined, (("ty", 0), ("tx", 1)), 1)
    box_slabs = (
        extended.reshape(9, channels, boxes_dev, BOX_PTS)
        .transpose(0, 2, 1, 3)
        .reshape(9 * boxes_dev, channels, BOX_PTS)
    )
    source_pts = box_slabs[:, :3]
    source_prb = box_slabs[:, 3:].astype(jnp.bfloat16)
    my_ty = lax.axis_index("ty")
    my_tx = lax.axis_index("tx")
    tile_cols = lax.axis_size("tx")
    slot_ids = near_boxes[0, 0]
    is_valid = slot_ids >= 0
    safe_ids = jnp.where(is_valid, slot_ids, 0)
    tile_idx = safe_ids // boxes_dev
    tile_row = tile_idx // tile_cols - my_ty + 1
    tile_col = tile_idx % tile_cols - my_tx + 1
    local_idx = jnp.where(is_valid, (tile_row * 3 + tile_col) * boxes_dev + safe_ids % boxes_dev, 0)
    own_points = points[0, 0].reshape(3, boxes_dev, BOX_PTS).transpose(1, 0, 2)

    def per_box(packed):
        target, slot_local, slot_ok = packed
        gathered_pts = source_pts[slot_local]
        gathered_prb = source_prb[slot_local] * slot_ok[:, None, None].astype(jnp.bfloat16)
        kernel = kernel_block(target, gathered_pts)
        return jnp.einsum("kts,kcs->ct", kernel, gathered_prb, preferred_element_type=jnp.float32)

    near_out = lax.map(per_box, (own_points, local_idx, is_valid))
    near_field = near_out.transpose(1, 0, 2).reshape(1, 1, near_out.shape[1], row_width)
    rank = leaf_bases.shape[2]
    basis_view = leaf_bases[0, 0].reshape(rank, boxes_dev, BOX_PTS)
    leaf_gram = jnp.einsum("rbp,sbp->brs", basis_view, basis_view, precision=lax.Precision.HIGHEST)
    leaf_factor = upper_factor(leaf_gram)
    stacked = jnp.einsum(
        "brs,bst->brt", leaf_factor, box_transfer[0, 0], precision=lax.Precision.HIGHEST
    )
    tile_gram = jnp.einsum("brt,bru->tu", stacked, stacked, precision=lax.Precision.HIGHEST)
    current = upper_factor(tile_gram)
    history = [current]
    level_idx = 0
    for bit_pos in range(lax.axis_size("tx").bit_length() - 1):
        side_bit = jnp.right_shift(my_tx, bit_pos) % 2
        own_transfer = jnp.where(
            side_bit == 0, upper_transfer[level_idx, 0], upper_transfer[level_idx, 1]
        )
        own_term = jnp.matmul(current, own_transfer, precision=lax.Precision.HIGHEST)
        partner = from_partner(own_term, "tx", bit_pos)
        current = upper_factor(gram_of(own_term) + gram_of(partner))
        history.append(current)
        level_idx = level_idx + 1
    for bit_pos in range(lax.axis_size("ty").bit_length() - 1):
        side_bit = jnp.right_shift(my_ty, bit_pos) % 2
        own_transfer = jnp.where(
            side_bit == 0, upper_transfer[level_idx, 0], upper_transfer[level_idx, 1]
        )
        own_term = jnp.matmul(current, own_transfer, precision=lax.Precision.HIGHEST)
        partner = from_partner(own_term, "ty", bit_pos)
        current = upper_factor(gram_of(own_term) + gram_of(partner))
        history.append(current)
        level_idx = level_idx + 1
    ancestors = jnp.stack(history, axis=0)[None, None]
    return (near_field, leaf_factor[None, None], ancestors)


def solution(mesh):
    return jax.shard_map(
        on_device,
        mesh=mesh,
        in_specs=(
            P("ty", "tx", None, None),
            P("ty", "tx", None, None),
            P("ty", "tx", None, None),
            P("ty", "tx", None, None),
            P("ty", "tx", None, None, None),
            P(),
        ),
        out_specs=(
            P("ty", "tx", None, None),
            P("ty", "tx", None, None, None),
            P("ty", "tx", None, None, None),
        ),
        check_vma=False,
    )
```

profile of v0, /device:TPU:6, one launch (start us, length us, event | category | flops | bytes accessed | tf_op | source)
XLA Modules:
  0.0 391.8 jit_solution(2926721376659389390)
XLA Ops:
  0.6 0.9 copy.82
  1.5 0.9 pad_maximum_fusion.2
  2.5 1.3 collective-permute-start.1
  3.8 3.0 collective-permute-start
  6.9 1.5 copy.148
  8.4 2.2 fusion.10
  11.0 93.8 %custom-call.6 = f32[16,64,64]{2,1,0:T(8,128)S(1)} custom-call(f32[16,64,64]{2,1,0:T(8,128)S(1)} %fusion.14), custom_call_target="Cholesky" | custom-call | tf_op jit(solution)/shard_map/jit(cholesky)/cholesky | solution.py:42
  105.0 1.1 fusion.12
  106.1 1.0 convolution_bitcast_fusion
  107.2 5.8 %cholesky.203 = f32[64,64]{1,0:T(8,128)S(1)} custom-call(f32[64,64]{1,0:T(8,128)S(1)} %fusion.47), custom_call_target="Cholesky" | custom-call | tf_op jit(solution)/shard_map/jit(cholesky)/cholesky | solution.py:42
  113.7 0.9 fusion.45
  114.6 3.5 collective-permute-start.4
  120.0 1.0 copy.118
  121.3 5.8 %cholesky.214 = f32[64,64]{1,0:T(8,128)S(1)} custom-call(f32[64,64]{1,0:T(8,128)S(1)} %fusion.44), custom_call_target="Cholesky" | custom-call | tf_op jit(solution)/shard_map/jit(cholesky)/cholesky | solution.py:42
  127.8 0.9 fusion.42
  129.0 4.5 %collective-permute-start.5 = (f32[64,64]{1,0:T(8,128)S(1)}, f32[64,64]{1,0:T(8,128)S(1)}, u32[]{:S(2)}, u32[]{:S(2)}) collective-permute-start(f32[64,64]{1,0:T(8,128)S(1)} %fusion.42), channel_id=1, source_target_pairs={{0,2},{1,3},{2,0},{3,1},{4,6},{5,7},{6,4},{7,5},{8,10},{9,11},{10,... | collective-permute-start | bytes 49160 | tf_op jit(solution)/shard_map/ppermute | solution.py:29
  134.1 1.5 collective-permute-done.5
  136.0 5.8 %cholesky.225 = f32[64,64]{1,0:T(8,128)S(1)} custom-call(f32[64,64]{1,0:T(8,128)S(1)} %fusion.41), custom_call_target="Cholesky" | custom-call | tf_op jit(solution)/shard_map/jit(cholesky)/cholesky | solution.py:42
  142.6 0.9 fusion.39
  143.7 7.3 %collective-permute-start.6 = (f32[64,64]{1,0:T(8,128)S(1)}, f32[64,64]{1,0:T(8,128)S(1)}, u32[]{:S(2)}, u32[]{:S(2)}) collective-permute-start(f32[64,64]{1,0:T(8,128)S(1)} %fusion.39), channel_id=1, source_target_pairs={{0,4},{1,5},{2,6},{3,7},{4,0},{5,1},{6,2},{7,3},{8,12},{9,13},{10,... | collective-permute-start | bytes 49160 | tf_op jit(solution)/shard_map/ppermute | solution.py:29
  151.7 2.1 collective-permute-done.6
  154.2 5.8 %cholesky.236 = f32[64,64]{1,0:T(8,128)S(1)} custom-call(f32[64,64]{1,0:T(8,128)S(1)} %fusion.38), custom_call_target="Cholesky" | custom-call | tf_op jit(solution)/shard_map/jit(cholesky)/cholesky | solution.py:42
  161.8 2.7 collective-permute-start.7
  165.2 2.4 collective-permute-done.7
  168.0 5.8 %cholesky.247 = f32[64,64]{1,0:T(8,128)S(1)} custom-call(f32[64,64]{1,0:T(8,128)S(1)} %fusion.35), custom_call_target="Cholesky" | custom-call | tf_op jit(solution)/shard_map/jit(cholesky)/cholesky | solution.py:42
  175.6 6.2 %collective-permute-start.8 = (f32[64,64]{1,0:T(8,128)S(1)}, f32[64,64]{1,0:T(8,128)S(1)}, u32[]{:S(2)}, u32[]{:S(2)}) collective-permute-start(f32[64,64]{1,0:T(8,128)S(1)} %fusion.33), channel_id=1, source_target_pairs={{0,16},{1,17},{2,18},{3,19},{4,20},{5,21},{6,22},{7,23},{8,24},{9,... | collective-permute-start | bytes 49160 | tf_op jit(solution)/shard_map/ppermute | solution.py:29
  182.5 1.2 collective-permute-done.8
  184.0 5.8 %cholesky.258 = f32[64,64]{1,0:T(8,128)S(1)} custom-call(f32[64,64]{1,0:T(8,128)S(1)} %fusion.32), custom_call_target="Cholesky" | custom-call | tf_op jit(solution)/shard_map/jit(cholesky)/cholesky | solution.py:42
  190.6 0.9 fusion.30
  191.7 1.9 collective-permute-start.9
  195.1 5.8 %cholesky.269 = f32[64,64]{1,0:T(8,128)S(1)} custom-call(f32[64,64]{1,0:T(8,128)S(1)} %fusion.29), custom_call_target="Cholesky" | custom-call | tf_op jit(solution)/shard_map/jit(cholesky)/cholesky | solution.py:42
  202.8 3.5 collective-permute-start.10
  207.0 1.6 collective-permute-done.10
  208.9 5.8 %cholesky.280 = f32[64,64]{1,0:T(8,128)S(1)} custom-call(f32[64,64]{1,0:T(8,128)S(1)} %fusion.26), custom_call_target="Cholesky" | custom-call | tf_op jit(solution)/shard_map/jit(cholesky)/cholesky | solution.py:42
  216.6 5.6 %collective-permute-start.11 = (f32[64,64]{1,0:T(8,128)S(1)}, f32[64,64]{1,0:T(8,128)S(1)}, u32[]{:S(2)}, u32[]{:S(2)}) collective-permute-start(f32[64,64]{1,0:T(8,128)S(1)} %fusion.24), channel_id=1, source_target_pairs={{0,128},{32,160},{64,192},{96,224},{128,0},{160,32},{192,64},{224,... | collective-permute-start | bytes 49160 | tf_op jit(solution)/shard_map/ppermute | solution.py:29
  222.9 1.3 collective-permute-done.11
  224.5 5.8 %cholesky.291 = f32[64,64]{1,0:T(8,128)S(1)} custom-call(f32[64,64]{1,0:T(8,128)S(1)} %fusion.23), custom_call_target="Cholesky" | custom-call | tf_op jit(solution)/shard_map/jit(cholesky)/cholesky | solution.py:42
  232.2 9.7 %collective-permute-start.12 = (f32[64,64]{1,0:T(8,128)S(1)}, f32[64,64]{1,0:T(8,128)S(1)}, u32[]{:S(2)}, u32[]{:S(2)}) collective-permute-start(f32[64,64]{1,0:T(8,128)S(1)} %fusion.21), channel_id=1, source_target_pairs={{0,256},{32,288},{64,320},{96,352},{128,384},{160,416},{192,448},{... | collective-permute-start | bytes 49160 | tf_op jit(solution)/shard_map/ppermute | solution.py:29
  242.6 1.2 collective-permute-done.12
  244.2 5.4 %collective-permute-start.3 = (f32[3,1,11,4096]{3,2,1,0:T(8,128)S(1)}, f32[3,1,11,4096]{3,2,1,0:T(8,128)}, u32[]{:S(2)}, u32[]{:S(2)}) collective-permute-start(f32[3,1,11,4096]{3,2,1,0:T(8,128)S(1)} %pad_maximum_fusion.1), channel_id=1, source_target_pairs={{1,0},{2,1},{3,2},{4,3},{5,4},{6,5},{7,6},{8,7},{9,8},{10,9},{11,1... | collective-permute-start | bytes 1622024 | tf_op jit(solution)/shard_map/ppermute | solution.py:21
  249.7 2.1 collective-permute-start.2
  251.8 5.8 %cholesky.302 = f32[64,64]{1,0:T(8,128)S(1)} custom-call(f32[64,64]{1,0:T(8,128)S(1)} %fusion.20), custom_call_target="Cholesky" | custom-call | tf_op jit(solution)/shard_map/jit(cholesky)/cholesky | solution.py:42
  259.9 3.7 collective-permute-done.3
  263.6 6.3 %collective-permute-done.2 = f32[3,1,11,4096]{3,2,1,0:T(8,128)} collective-permute-done((f32[3,1,11,4096]{3,2,1,0:T(8,128)S(1)}, f32[3,1,11,4096]{3,2,1,0:T(8,128)}, u32[]{:S(2)}, u32[]{:S(2)}) %collective-permute-start.2) | collective-permute-done | bytes 540704 | tf_op jit(solution)/shard_map/ppermute | solution.py:20
  269.9 1.7 pad_maximum_fusion
  271.6 1.6 reshape.90
  273.2 2.4 copy.83
  275.9 115.2 %while.10 = (s32[]{:T(128)}, f32[16,8,256]{2,1,0:T(8,128)S(1)}, s32[16,27]{1,0:T(8,128)S(1)}, bf16[144,8,256]{2,1,0:T(8,128)(2,1)S(1)}, pred[16,27]{1,0:T(8,128)...) while((s32[]{:T(128)}, f32[16,8,256]{2,1,0:T(8,128)S(1)}, ...), condition=%wide.region_1.2_spmd, body=%wide.region_0.1_spmd.sunk | while | flops 51371120 | bytes 950546 | solution.py:81
  278.0 5.1 %fusion.203 = f32[16,8,256]{2,1,0:T(8,128)S(1)} fusion(f32[16,8,256]{2,1,0:T(8,128)S(1)} %get-tuple-element.158, s32[]{:T(128)S(6)} %copy.164, f32[27,256]{1,0:T(8,128)S(1)} %get-tuple-element.140, f32[256]{0:T(256)S(1)} %bitcast.242, f32[27,256]{1,0:T(8,128)S(1)} %get-tuple-element.142, f32[256]{0:T(256)S(1)} %bitcast.241, ...), kind=kOutput, calls=%fused_computation.5.clone.1 | convolution fusion | flops 51369984 | bytes 220676 | tf_op jit(solution)/shard_map/while/body/eval_jaxpr/kts,kcs->ct/dot_general | solution.py:79
  285.2 5.1 %fusion.203 = f32[16,8,256]{2,1,0:T(8,128)S(1)} fusion(f32[16,8,256]{2,1,0:T(8,128)S(1)} %get-tuple-element.158, s32[]{:T(128)S(6)} %copy.164, f32[27,256]{1,0:T(8,128)S(1)} %get-tuple-element.140, f32[256]{0:T(256)S(1)} %bitcast.242, f32[27,256]{1,0:T(8,128)S(1)} %get-tuple-element.142, f32[256]{0:T(256)S(1)} %bitcast.241, ...), kind=kOutput, calls=%fused_computation.5.clone.1 | convolution fusion | flops 51369984 | bytes 220676 | tf_op jit(solution)/shard_map/while/body/eval_jaxpr/kts,kcs->ct/dot_general | solution.py:79
  292.4 5.1 %fusion.203 = f32[16,8,256]{2,1,0:T(8,128)S(1)} fusion(f32[16,8,256]{2,1,0:T(8,128)S(1)} %get-tuple-element.158, s32[]{:T(128)S(6)} %copy.164, f32[27,256]{1,0:T(8,128)S(1)} %get-tuple-element.140, f32[256]{0:T(256)S(1)} %bitcast.242, f32[27,256]{1,0:T(8,128)S(1)} %get-tuple-element.142, f32[256]{0:T(256)S(1)} %bitcast.241, ...), kind=kOutput, calls=%fused_computation.5.clone.1 | convolution fusion | flops 51369984 | bytes 220676 | tf_op jit(solution)/shard_map/while/body/eval_jaxpr/kts,kcs->ct/dot_general | solution.py:79
  299.6 5.1 %fusion.203 = f32[16,8,256]{2,1,0:T(8,128)S(1)} fusion(f32[16,8,256]{2,1,0:T(8,128)S(1)} %get-tuple-element.158, s32[]{:T(128)S(6)} %copy.164, f32[27,256]{1,0:T(8,128)S(1)} %get-tuple-element.140, f32[256]{0:T(256)S(1)} %bitcast.242, f32[27,256]{1,0:T(8,128)S(1)} %get-tuple-element.142, f32[256]{0:T(256)S(1)} %bitcast.241, ...), kind=kOutput, calls=%fused_computation.5.clone.1 | convolution fusion | flops 51369984 | bytes 220676 | tf_op jit(solution)/shard_map/while/body/eval_jaxpr/kts,kcs->ct/dot_general | solution.py:79
  306.8 5.1 %fusion.203 = f32[16,8,256]{2,1,0:T(8,128)S(1)} fusion(f32[16,8,256]{2,1,0:T(8,128)S(1)} %get-tuple-element.158, s32[]{:T(128)S(6)} %copy.164, f32[27,256]{1,0:T(8,128)S(1)} %get-tuple-element.140, f32[256]{0:T(256)S(1)} %bitcast.242, f32[27,256]{1,0:T(8,128)S(1)} %get-tuple-element.142, f32[256]{0:T(256)S(1)} %bitcast.241, ...), kind=kOutput, calls=%fused_computation.5.clone.1 | convolution fusion | flops 51369984 | bytes 220676 | tf_op jit(solution)/shard_map/while/body/eval_jaxpr/kts,kcs->ct/dot_general | solution.py:79
  314.0 5.1 %fusion.203 = f32[16,8,256]{2,1,0:T(8,128)S(1)} fusion(f32[16,8,256]{2,1,0:T(8,128)S(1)} %get-tuple-element.158, s32[]{:T(128)S(6)} %copy.164, f32[27,256]{1,0:T(8,128)S(1)} %get-tuple-element.140, f32[256]{0:T(256)S(1)} %bitcast.242, f32[27,256]{1,0:T(8,128)S(1)} %get-tuple-element.142, f32[256]{0:T(256)S(1)} %bitcast.241, ...), kind=kOutput, calls=%fused_computation.5.clone.1 | convolution fusion | flops 51369984 | bytes 220676 | tf_op jit(solution)/shard_map/while/body/eval_jaxpr/kts,kcs->ct/dot_general | solution.py:79
  321.2 5.1 %fusion.203 = f32[16,8,256]{2,1,0:T(8,128)S(1)} fusion(f32[16,8,256]{2,1,0:T(8,128)S(1)} %get-tuple-element.158, s32[]{:T(128)S(6)} %copy.164, f32[27,256]{1,0:T(8,128)S(1)} %get-tuple-element.140, f32[256]{0:T(256)S(1)} %bitcast.242, f32[27,256]{1,0:T(8,128)S(1)} %get-tuple-element.142, f32[256]{0:T(256)S(1)} %bitcast.241, ...), kind=kOutput, calls=%fused_computation.5.clone.1 | convolution fusion | flops 51369984 | bytes 220676 | tf_op jit(solution)/shard_map/while/body/eval_jaxpr/kts,kcs->ct/dot_general | solution.py:79
  328.4 5.1 %fusion.203 = f32[16,8,256]{2,1,0:T(8,128)S(1)} fusion(f32[16,8,256]{2,1,0:T(8,128)S(1)} %get-tuple-element.158, s32[]{:T(128)S(6)} %copy.164, f32[27,256]{1,0:T(8,128)S(1)} %get-tuple-element.140, f32[256]{0:T(256)S(1)} %bitcast.242, f32[27,256]{1,0:T(8,128)S(1)} %get-tuple-element.142, f32[256]{0:T(256)S(1)} %bitcast.241, ...), kind=kOutput, calls=%fused_computation.5.clone.1 | convolution fusion | flops 51369984 | bytes 220676 | tf_op jit(solution)/shard_map/while/body/eval_jaxpr/kts,kcs->ct/dot_general | solution.py:79
  335.6 5.1 %fusion.203 = f32[16,8,256]{2,1,0:T(8,128)S(1)} fusion(f32[16,8,256]{2,1,0:T(8,128)S(1)} %get-tuple-element.158, s32[]{:T(128)S(6)} %copy.164, f32[27,256]{1,0:T(8,128)S(1)} %get-tuple-element.140, f32[256]{0:T(256)S(1)} %bitcast.242, f32[27,256]{1,0:T(8,128)S(1)} %get-tuple-element.142, f32[256]{0:T(256)S(1)} %bitcast.241, ...), kind=kOutput, calls=%fused_computation.5.clone.1 | convolution fusion | flops 51369984 | bytes 220676 | tf_op jit(solution)/shard_map/while/body/eval_jaxpr/kts,kcs->ct/dot_general | solution.py:79
  342.9 5.1 %fusion.203 = f32[16,8,256]{2,1,0:T(8,128)S(1)} fusion(f32[16,8,256]{2,1,0:T(8,128)S(1)} %get-tuple-element.158, s32[]{:T(128)S(6)} %copy.164, f32[27,256]{1,0:T(8,128)S(1)} %get-tuple-element.140, f32[256]{0:T(256)S(1)} %bitcast.242, f32[27,256]{1,0:T(8,128)S(1)} %get-tuple-element.142, f32[256]{0:T(256)S(1)} %bitcast.241, ...), kind=kOutput, calls=%fused_computation.5.clone.1 | convolution fusion | flops 51369984 | bytes 220676 | tf_op jit(solution)/shard_map/while/body/eval_jaxpr/kts,kcs->ct/dot_general | solution.py:79
  350.1 5.1 %fusion.203 = f32[16,8,256]{2,1,0:T(8,128)S(1)} fusion(f32[16,8,256]{2,1,0:T(8,128)S(1)} %get-tuple-element.158, s32[]{:T(128)S(6)} %copy.164, f32[27,256]{1,0:T(8,128)S(1)} %get-tuple-element.140, f32[256]{0:T(256)S(1)} %bitcast.242, f32[27,256]{1,0:T(8,128)S(1)} %get-tuple-element.142, f32[256]{0:T(256)S(1)} %bitcast.241, ...), kind=kOutput, calls=%fused_computation.5.clone.1 | convolution fusion | flops 51369984 | bytes 220676 | tf_op jit(solution)/shard_map/while/body/eval_jaxpr/kts,kcs->ct/dot_general | solution.py:79
  357.3 5.1 %fusion.203 = f32[16,8,256]{2,1,0:T(8,128)S(1)} fusion(f32[16,8,256]{2,1,0:T(8,128)S(1)} %get-tuple-element.158, s32[]{:T(128)S(6)} %copy.164, f32[27,256]{1,0:T(8,128)S(1)} %get-tuple-element.140, f32[256]{0:T(256)S(1)} %bitcast.242, f32[27,256]{1,0:T(8,128)S(1)} %get-tuple-element.142, f32[256]{0:T(256)S(1)} %bitcast.241, ...), kind=kOutput, calls=%fused_computation.5.clone.1 | convolution fusion | flops 51369984 | bytes 220676 | tf_op jit(solution)/shard_map/while/body/eval_jaxpr/kts,kcs->ct/dot_general | solution.py:79
  364.5 5.1 %fusion.203 = f32[16,8,256]{2,1,0:T(8,128)S(1)} fusion(f32[16,8,256]{2,1,0:T(8,128)S(1)} %get-tuple-element.158, s32[]{:T(128)S(6)} %copy.164, f32[27,256]{1,0:T(8,128)S(1)} %get-tuple-element.140, f32[256]{0:T(256)S(1)} %bitcast.242, f32[27,256]{1,0:T(8,128)S(1)} %get-tuple-element.142, f32[256]{0:T(256)S(1)} %bitcast.241, ...), kind=kOutput, calls=%fused_computation.5.clone.1 | convolution fusion | flops 51369984 | bytes 220676 | tf_op jit(solution)/shard_map/while/body/eval_jaxpr/kts,kcs->ct/dot_general | solution.py:79
  371.7 5.1 %fusion.203 = f32[16,8,256]{2,1,0:T(8,128)S(1)} fusion(f32[16,8,256]{2,1,0:T(8,128)S(1)} %get-tuple-element.158, s32[]{:T(128)S(6)} %copy.164, f32[27,256]{1,0:T(8,128)S(1)} %get-tuple-element.140, f32[256]{0:T(256)S(1)} %bitcast.242, f32[27,256]{1,0:T(8,128)S(1)} %get-tuple-element.142, f32[256]{0:T(256)S(1)} %bitcast.241, ...), kind=kOutput, calls=%fused_computation.5.clone.1 | convolution fusion | flops 51369984 | bytes 220676 | tf_op jit(solution)/shard_map/while/body/eval_jaxpr/kts,kcs->ct/dot_general | solution.py:79
  378.9 5.1 %fusion.203 = f32[16,8,256]{2,1,0:T(8,128)S(1)} fusion(f32[16,8,256]{2,1,0:T(8,128)S(1)} %get-tuple-element.158, s32[]{:T(128)S(6)} %copy.164, f32[27,256]{1,0:T(8,128)S(1)} %get-tuple-element.140, f32[256]{0:T(256)S(1)} %bitcast.242, f32[27,256]{1,0:T(8,128)S(1)} %get-tuple-element.142, f32[256]{0:T(256)S(1)} %bitcast.241, ...), kind=kOutput, calls=%fused_computation.5.clone.1 | convolution fusion | flops 51369984 | bytes 220676 | tf_op jit(solution)/shard_map/while/body/eval_jaxpr/kts,kcs->ct/dot_general | solution.py:79
  386.1 5.1 %fusion.203 = f32[16,8,256]{2,1,0:T(8,128)S(1)} fusion(f32[16,8,256]{2,1,0:T(8,128)S(1)} %get-tuple-element.158, s32[]{:T(128)S(6)} %copy.164, f32[27,256]{1,0:T(8,128)S(1)} %get-tuple-element.140, f32[256]{0:T(256)S(1)} %bitcast.242, f32[27,256]{1,0:T(8,128)S(1)} %get-tuple-element.142, f32[256]{0:T(256)S(1)} %bitcast.241, ...), kind=kOutput, calls=%fused_computation.5.clone.1 | convolution fusion | flops 51369984 | bytes 220676 | tf_op jit(solution)/shard_map/while/body/eval_jaxpr/kts,kcs->ct/dot_general | solution.py:79
  (253 shorter events, 59.1 us)
Async XLA Ops:
  0.6 104.3 %copy-start = (f32[1,1,16,64,64]{4,3,2,1,0:T(8,128)S(1)}, f32[1,1,16,64,64]{4,3,2,1,0:T(8,128)}, u32[]{:S(2)}) copy-start(f32[1,1,16,64,64]{4,3,2,1,0:T(8,128)} %param.13) | copy-start | bytes 786436
  2.5 241.6 %collective-permute-start.1 = (f32[1,1,11,4096]{3,2,1,0:T(8,128)S(1)}, f32[1,1,11,4096]{3,2,1,0:T(8,128)S(1)}, u32[]{:S(2)}, u32[]{:S(2)}) collective-permute-start(f32[1,1,11,4096]{3,2,1,0:T(8,128)S(1)} %pad_maximum_fusion.2), channel_id=1, source_target_pairs={{32,0},{64,32},{96,64},{128,96},{160,128},{192,160},{224,192},{256... | collective-permute-start | bytes 540680 | tf_op jit(solution)/shard_map/ppermute | solution.py:21
  3.8 240.4 %collective-permute-start = (f32[1,1,11,4096]{3,2,1,0:T(8,128)S(1)}, f32[1,1,11,4096]{3,2,1,0:T(8,128)S(1)}, u32[]{:S(2)}, u32[]{:S(2)}) collective-permute-start(f32[1,1,11,4096]{3,2,1,0:T(8,128)S(1)} %pad_maximum_fusion.2), channel_id=1, source_target_pairs={{0,32},{32,64},{64,96},{96,128},{128,160},{160,192},{192,224},{224... | collective-permute-start | bytes 540680 | tf_op jit(solution)/shard_map/ppermute | solution.py:20
  10.9 102.8 %copy-start.4 = (f32[9,2,64,64]{3,2,1,0:T(8,128)S(1)}, f32[9,2,64,64]{3,2,1,0:T(8,128)}, u32[]{:S(2)}) copy-start(f32[9,2,64,64]{3,2,1,0:T(8,128)} %param.14) | copy-start | bytes 884740
  104.7 14.4 %copy-start.5 = (s32[1,1,16,27]{3,2,1,0:T(8,128)S(1)}, s32[1,1,16,27]{3,2,1,0:T(8,128)}, u32[]{:S(2)}) copy-start(s32[1,1,16,27]{3,2,1,0:T(8,128)} %param.11) | copy-start | bytes 5188
  104.8 14.5 %copy-start.3 = (f32[1,1,3,4096]{3,1,2,0:T(1,128)S(1)}, f32[1,1,3,4096]{3,1,2,0:T(1,128)}, u32[]{:S(2)}) copy-start(f32[1,1,3,4096]{3,1,2,0:T(1,128)} %param.9) | copy-start | bytes 147460
  114.6 6.4 %collective-permute-start.4 = (f32[64,64]{1,0:T(8,128)S(1)}, f32[64,64]{1,0:T(8,128)S(1)}, u32[]{:S(2)}, u32[]{:S(2)}) collective-permute-start(f32[64,64]{1,0:T(8,128)S(1)} %fusion.45), channel_id=1, source_target_pairs={{0,1},{1,0},{2,3},{3,2},{4,5},{5,4},{6,7},{7,6},{8,9},{9,8},{10,11... | collective-permute-start | bytes 49160 | tf_op jit(solution)/shard_map/ppermute | solution.py:29
  121.3 122.8 %copy-start.1 = (f32[1,1,8,4096]{3,2,1,0:T(8,128)S(1)}, f32[1,1,8,4096]{3,2,1,0:T(8,128)}, u32[]{:S(2)}) copy-start(f32[1,1,8,4096]{3,2,1,0:T(8,128)} %param.10) | copy-start | bytes 393220
  129.0 6.7 %collective-permute-start.5 = (f32[64,64]{1,0:T(8,128)S(1)}, f32[64,64]{1,0:T(8,128)S(1)}, u32[]{:S(2)}, u32[]{:S(2)}) collective-permute-start(f32[64,64]{1,0:T(8,128)S(1)} %fusion.42), channel_id=1, source_target_pairs={{0,2},{1,3},{2,0},{3,1},{4,6},{5,7},{6,4},{7,5},{8,10},{9,11},{10,... | collective-permute-start | bytes 49160 | tf_op jit(solution)/shard_map/ppermute | solution.py:29
  143.7 10.1 %collective-permute-start.6 = (f32[64,64]{1,0:T(8,128)S(1)}, f32[64,64]{1,0:T(8,128)S(1)}, u32[]{:S(2)}, u32[]{:S(2)}) collective-permute-start(f32[64,64]{1,0:T(8,128)S(1)} %fusion.39), channel_id=1, source_target_pairs={{0,4},{1,5},{2,6},{3,7},{4,0},{5,1},{6,2},{7,3},{8,12},{9,13},{10,... | collective-permute-start | bytes 49160 | tf_op jit(solution)/shard_map/ppermute | solution.py:29
  161.8 5.8 %collective-permute-start.7 = (f32[64,64]{1,0:T(8,128)S(1)}, f32[64,64]{1,0:T(8,128)S(1)}, u32[]{:S(2)}, u32[]{:S(2)}) collective-permute-start(f32[64,64]{1,0:T(8,128)S(1)} %fusion.36), channel_id=1, source_target_pairs={{0,8},{1,9},{2,10},{3,11},{4,12},{5,13},{6,14},{7,15},{8,0},{9,1},... | collective-permute-start | bytes 49160 | tf_op jit(solution)/shard_map/ppermute | solution.py:29
  175.6 8.1 %collective-permute-start.8 = (f32[64,64]{1,0:T(8,128)S(1)}, f32[64,64]{1,0:T(8,128)S(1)}, u32[]{:S(2)}, u32[]{:S(2)}) collective-permute-start(f32[64,64]{1,0:T(8,128)S(1)} %fusion.33), channel_id=1, source_target_pairs={{0,16},{1,17},{2,18},{3,19},{4,20},{5,21},{6,22},{7,23},{8,24},{9,... | collective-permute-start | bytes 49160 | tf_op jit(solution)/shard_map/ppermute | solution.py:29
  191.7 3.1 collective-permute-start.9
  202.8 5.8 %collective-permute-start.10 = (f32[64,64]{1,0:T(8,128)S(1)}, f32[64,64]{1,0:T(8,128)S(1)}, u32[]{:S(2)}, u32[]{:S(2)}) collective-permute-start(f32[64,64]{1,0:T(8,128)S(1)} %fusion.27), channel_id=1, source_target_pairs={{0,64},{32,96},{64,0},{96,32},{128,192},{160,224},{192,128},{224,1... | collective-permute-start | bytes 49160 | tf_op jit(solution)/shard_map/ppermute | solution.py:29
  216.6 7.6 %collective-permute-start.11 = (f32[64,64]{1,0:T(8,128)S(1)}, f32[64,64]{1,0:T(8,128)S(1)}, u32[]{:S(2)}, u32[]{:S(2)}) collective-permute-start(f32[64,64]{1,0:T(8,128)S(1)} %fusion.24), channel_id=1, source_target_pairs={{0,128},{32,160},{64,192},{96,224},{128,0},{160,32},{192,64},{224,... | collective-permute-start | bytes 49160 | tf_op jit(solution)/shard_map/ppermute | solution.py:29
  232.2 11.6 %collective-permute-start.12 = (f32[64,64]{1,0:T(8,128)S(1)}, f32[64,64]{1,0:T(8,128)S(1)}, u32[]{:S(2)}, u32[]{:S(2)}) collective-permute-start(f32[64,64]{1,0:T(8,128)S(1)} %fusion.21), channel_id=1, source_target_pairs={{0,256},{32,288},{64,320},{96,352},{128,384},{160,416},{192,448},{... | collective-permute-start | bytes 49160 | tf_op jit(solution)/shard_map/ppermute | solution.py:29
  244.2 19.5 %copy-start.2 = (f32[1,1,11,4096]{3,2,1,0:T(8,128)}, f32[1,1,11,4096]{3,2,1,0:T(8,128)S(1)}, u32[]{:S(2)}) copy-start(f32[1,1,11,4096]{3,2,1,0:T(8,128)S(1)} %collective-permute-done) | copy-start | bytes 540676
  244.2 19.4 %collective-permute-start.3 = (f32[3,1,11,4096]{3,2,1,0:T(8,128)S(1)}, f32[3,1,11,4096]{3,2,1,0:T(8,128)}, u32[]{:S(2)}, u32[]{:S(2)}) collective-permute-start(f32[3,1,11,4096]{3,2,1,0:T(8,128)S(1)} %pad_maximum_fusion.1), channel_id=1, source_target_pairs={{1,0},{2,1},{3,2},{4,3},{5,4},{6,5},{7,6},{8,7},{9,8},{10,9},{11,1... | collective-permute-start | bytes 1622024 | tf_op jit(solution)/shard_map/ppermute | solution.py:21
  249.7 20.3 %collective-permute-start.2 = (f32[3,1,11,4096]{3,2,1,0:T(8,128)S(1)}, f32[3,1,11,4096]{3,2,1,0:T(8,128)}, u32[]{:S(2)}, u32[]{:S(2)}) collective-permute-start(f32[3,1,11,4096]{3,2,1,0:T(8,128)S(1)} %pad_maximum_fusion.1), channel_id=1, source_target_pairs={{0,1},{1,2},{2,3},{3,4},{4,5},{5,6},{6,7},{7,8},{8,9},{9,10},{10,1... | collective-permute-start | bytes 1622024 | tf_op jit(solution)/shard_map/ppermute | solution.py:20
  273.2 2.8 copy-start.6
  391.2 0.7 copy-start.7
where the time goes:
time: 394 us; the launch traced here: 392 us
  other arithmetic  169 us (43%)
  matrix products  98.4 us (25%)
  starting transfers between devices  56.9 us (14%)
  local copies, waits for them, and re-layouts  42.9 us (11%)
  waiting for transfers between devices  22.1 us (6%)
    another operation x34, other arithmetic, upper_factor(): return jnp.swapaxes(jnp.linalg.cholesky(gram_sum), -1, -2)  159 us
    dot_general x16, matrix products, per_box(): jnp.einsum('kts,kcs->ct', kernel, gathered_prb, preferred_element_type=jn...  81.9 us
    ppermute x9, starting transfers between devices, from_partner(): return lax.ppermute(value, axis, pairs)  44.9 us
    slice x32, local copies, waits for them, and re-layouts, kernel_block(): delta = target[coord][None, :, None] - source[:, coord][:, None, :]  12.9 us
    ppermute x9, waiting for transfers between devices, from_partner(): return lax.ppermute(value, axis, pairs)  12 us
    gather x16, local copies, waits for them, and re-layouts, per_box(): gathered_pts = source_pts[slot_local]  9.88 us
    gather x16, local copies, waits for them, and re-layouts, per_box(): source_prb[slot_local] * slot_ok[:, None, None].astype(jnp.bfloat16)  9.07 us
    dot_general x9, matrix products, on_device(): jnp.matmul(current, own_transfer, precision=lax.Precision.HIGHEST)  7.92 us
  transfers between devices with their start and end apart: 13, of which 10 were waited for; matrix products, arithmetic and copies ran while one was open for 48% of the time, Pallas kernels for 0%

commit v1 on v0

v1 whole, which is shorter than its diff:
```python
import functools
import math

import jax
import jax.numpy as jnp
from jax import lax
from jax.experimental import pallas as pl
from jax.experimental.pallas import tpu as pltpu
from jax.sharding import PartitionSpec as P

MESH = pl.DeviceIdType.MESH
HIGHEST = lax.Precision.HIGHEST
F32, BF16 = jnp.float32, jnp.bfloat16
LN2 = math.log(2.0)
ALPHA = math.sqrt(3.0) / LN2
BOXES, PTS, RANK = 16, 256, 64
COLUMNS = ((0, 1), (0, 0), (1, 0), (1, 1))
BOX_AT = tuple(x + 2 * y + 4 * z for x, y in COLUMNS for z in range(4))
HALO = ((0, -1, 4, 8, 0), (-1, 0, 0, 8, 8), (-1, -1, 4, 4, 16), (-1, 1, 0, 4, 20))
REMOTE = 24
Z_PAIRS = tuple((a, b) for a in range(4) for b in range(4) if abs(a - b) <= 1)


def dot(a, b, ca, cb, precision=None):
    return lax.dot_general(
        a, b, (((ca,), (cb,)), ((), ())), precision=precision, preferred_element_type=F32
    )


def split3(value):
    high = value.astype(BF16).astype(F32)
    rest = value - high
    mid = rest.astype(BF16).astype(F32)
    return high, mid, (rest - mid).astype(BF16).astype(F32)


def features(rows, center, left):
    sub = lax.broadcasted_iota(jnp.int32, rows.shape, 0)
    cy, cx = center
    mid = jnp.where(sub == 0, cy, jnp.where(sub == 1, cx, 2.0))
    y = jnp.where(sub < 3, (rows - mid) * ALPHA, 0.0)
    norm = jnp.sum(y * y, axis=0, keepdims=True)
    zero = jnp.zeros_like(y)
    if left:
        h, m, l = split3(jnp.where(sub == 3, norm, y))
        one = jnp.where(sub == 4, 1.0, 0.0)
        coord = lambda v: jnp.where(sub < 3, -2.0 * v, 0.0)
        lead = lambda c, n: jnp.where(sub < 3, -2.0 * c, jnp.where(sub == 3, n, one))
        parts = (lead(h, h), lead(h, m), lead(m, l), coord(m), coord(h), coord(l))
    else:
        h, m, l = split3(jnp.where(sub == 4, norm, y))
        one = jnp.where(sub == 3, 1.0, 0.0)
        parts = (h + one, m + one, jnp.where(sub < 3, h, l) + one, m, l, h)
    return jnp.concatenate(parts, axis=0).astype(BF16)


def matern(square):
    s = jnp.maximum(square, 1e-12)
    u = s * lax.rsqrt(s)
    return ((1.0 + LN2 * u) * jnp.exp2(-u)).astype(BF16)


def halves(packed):
    return jnp.concatenate([packed[:, :RANK], packed[:, RANK:]], axis=0)


def packed(full):
    return jnp.concatenate([full[:32], full[32:]], axis=1)


def remote(src, dst, send, recv, device, comm):
    if comm:
        return pltpu.make_async_remote_copy(
            src_ref=src, dst_ref=dst, send_sem=send, recv_sem=recv, device_id=device, device_id_type=MESH
        )
    return None


def main_kernel(sizes, comm, pts, prb, near, leaf, trans, upper, near_out, gram_out,
                box, left, right, mask, acc, back, kern, grams, tree_out, tree_in,
                halo_send, halo_recv, back_send, back_recv, tree_send, tree_recv):
    n_ty, n_tx = sizes
    ty, tx = (lax.axis_index("ty"), lax.axis_index("tx")) if comm else (jnp.int32(0), jnp.int32(0))
    center = ((2 * ty + 1).astype(F32), (2 * tx + 1).astype(F32))

    def at(dy, dx):
        return (lax.rem(ty + dy + n_ty, n_ty), lax.rem(tx + dx + n_tx, n_tx))

    bits = [lax.rem(tx // 2**i, 2) for i in range(5)] + [lax.rem(ty // 2**i, 2) for i in range(4)]

    def relative(level, q):
        row, col = ty, tx
        for i in range(3):
            if q >> i & 1:
                b = level + i
                if b < 5:
                    col = col + 2**b * (1 - 2 * bits[b])
                else:
                    row = row + 2 ** (b - 5) * (1 - 2 * bits[b])
        return (row, col)

    peers = [at(*h[:2]) for h in HALO] + [at(-h[0], -h[1]) for h in HALO]
    peers += [relative(3 * r, q) for r in range(3) for q in range(1, 8)]
    if comm:
        barrier = pltpu.get_barrier_semaphore()
        for peer in peers:
            pl.semaphore_signal(barrier, inc=1, device_id=peer, device_id_type=MESH)

    for i, k in enumerate(BOX_AT):
        cols = slice(k * PTS, (k + 1) * PTS)
        box[i, 0:3, :] = pts[0, 0, :, cols]
        box[i, 8:16, :] = prb[0, 0, :, cols]
        box[i, 3:8, :] = jnp.zeros((5, PTS), F32)
        box[i, 3:4, 0:27] = jnp.where(near[0, 0, k : k + 1, :] >= 0, 1.0, 0.0)

    if comm:
        pl.semaphore_wait(barrier, len(peers))

    def halo(j):
        dy, dx, first, count, row = HALO[j]
        src, dst = box.at[pl.ds(first, count)], box.at[pl.ds(BOXES + row, count)]
        if comm:
            return pltpu.make_async_remote_copy(
                src_ref=src, dst_ref=dst, send_sem=halo_send.at[j], recv_sem=halo_recv.at[j],
                device_id=at(dy, dx), device_id_type=MESH)
        return pltpu.make_async_copy(src, dst, halo_recv.at[j])

    def reply(j):
        dy, dx, first, count, row = HALO[j]
        src, dst = acc.at[pl.ds(BOXES + row, count)], back.at[pl.ds(row, count)]
        if comm:
            return pltpu.make_async_remote_copy(
                src_ref=src, dst_ref=dst, send_sem=back_send.at[j], recv_sem=back_recv.at[j],
                device_id=at(-dy, -dx), device_id_type=MESH)
        return pltpu.make_async_copy(src, dst, back_recv.at[j])

    def exchange(r, q):
        count = 3 if q == 1 else 2 if q < 4 else 1
        src, dst = tree_out.at[r, pl.ds(0, count)], tree_in.at[r, q - 1, pl.ds(0, count)]
        j = 7 * r + q - 1
        if comm:
            return pltpu.make_async_remote_copy(
                src_ref=src, dst_ref=dst, send_sem=tree_send.at[j], recv_sem=tree_recv.at[j],
                device_id=relative(3 * r, q), device_id_type=MESH)
        return pltpu.make_async_copy(src, dst, tree_recv.at[j])

    def wait_send(copy):
        if comm:
            copy.wait_send()

    def wait_recv(copy):
        if comm:
            copy.wait_recv()
        else:
            copy.wait()

    for j in range(4):
        halo(j).start()

    total = jnp.zeros((RANK, RANK), F32)
    pair = []
    for k in range(BOXES):
        v = leaf[0, 0, :, k * PTS : (k + 1) * PTS]
        stack = jnp.concatenate(split3(v), axis=0).astype(BF16)
        c = dot(stack, stack, 1, 1)
        g = c[128:, :64] + c[:64, 128:] + c[64:128, 64:128]
        g = g + (c[:64, 64:128] + c[64:128, :64]) + c[:64, :64]
        pair.append(g)
        if k % 2:
            gram_out[k // 2] = jnp.concatenate(pair, axis=1)
            pair = []
        t = trans[0, 0, k]
        total = total + dot(t, dot(g, t, 1, 0, HIGHEST), 0, 0, HIGHEST)
    grams[0] = total

    def send_round(r):
        node = grams[3 * r]
        path = None
        for i in range(3):
            step = upper[3 * r + i, bits[3 * r + i]]
            path = step if path is None else dot(path, step, 1, 0, HIGHEST)
            term = dot(path, dot(node, path, 1, 0, HIGHEST), 0, 0, HIGHEST)
            tree_out[r, 2 - i] = packed(term)
        for q in range(1, 8):
            exchange(r, q).start()

    def finish_round(r):
        for q in range(1, 8):
            wait_recv(exchange(r, q))
        for i in range(3):
            node = tree_out[r, 2 - i]
            for q in range(1, 2 ** (i + 1)):
                node = node + tree_in[r, q - 1, 2 - i]
            grams[3 * r + i + 1] = halves(node)

    send_round(0)

    lane = lax.broadcasted_iota(jnp.int32, (32, 128), 1)
    row = lax.broadcasted_iota(jnp.int32, (32, 128), 0)
    ones = jnp.ones((128, 128), BF16)
    diag = lax.broadcasted_iota(jnp.int32, (PTS, PTS), 0) == lax.broadcasted_iota(jnp.int32, (PTS, PTS), 1)
    eye = jnp.where(diag, 1.0, 0.0).astype(BF16)

    def prepare(i, own):
        rows = box[i, 0:8, :]
        right[i] = features(rows, center, False)
        if own:
            left[i] = dot(eye, features(rows, center, True), 1, 1).astype(BF16)
        slots = jnp.where(lane == row, box[i, 3:4, 0:128], 0.0).astype(BF16)
        mask[i] = dot(slots, ones, 1, 0)
        acc[i] = jnp.zeros((8, PTS), F32)

    def loop(n, body):
        lax.fori_loop(0, n, lambda i, c: (body(i), c)[1], 0)

    def probe(i, owner, slot):
        m = mask[owner, pl.ds(slot, 1), :]
        return (box[i, 8:16, :] * jnp.concatenate([m, m], axis=1)).astype(BF16)

    def blocks(a0, b0, step, pairs, one_sided=()):
        sums = {}

        def first(m, za, zb):
            kern[m] = matern(dot(left[a0 + za], right[b0 + zb], 1, 0))

        def add(key, value):
            sums[key] = value if key not in sums else sums[key] + value

        def second(m, za, zb):
            block = kern[m]
            a, b = a0 + za, b0 + zb
            slot = 13 + step + (zb - za)
            add(("a", za), dot(probe(b, a, slot), block, 1, 1))
            if (za, zb) not in one_sided:
                add(("b", zb), dot(probe(a, b, 26 - slot), block, 1, 0))

        late = 2
        for m in range(len(pairs) + late):
            if m < len(pairs):
                first(m, *pairs[m])
            if m >= late:
                second(m - late, *pairs[m - late])
        for (side, z), value in sums.items():
            at_box = (a0 if side == "a" else b0) + z
            acc[at_box] = acc[at_box] + value

    loop(BOXES, lambda i: prepare(i, True))

    def own_pair(i):
        d, j = i // 2 + 1, lax.rem(i, 2)
        a = j * (1 + 1 // d)
        b = a + d - 2 * a * (d // 3)
        x = lambda p: p // 2
        y = lambda p: 1 - lax.rem((p + 1) // 2, 2)
        blocks(4 * a, 4 * b, 9 * (x(b) - x(a)) + 3 * (y(b) - y(a)), Z_PAIRS)

    def tx_pair(i):
        xa, xb = lax.rem(i, 2), i // 2
        blocks(12 * xa, BOXES + 4 * xb, 9 * (xb - xa) + 3, Z_PAIRS)

    def ty_pair(i):
        ya, p = lax.rem(i, 2), i // 2
        blocks(8 + 4 * ya, BOXES + 8 + 4 * p, 9 + 3 * (1 - p - ya), Z_PAIRS)

    def corner_pair(i):
        blocks(12 - 4 * i, BOXES + 16 + 4 * i, 9 + 3 * (1 - 2 * i), Z_PAIRS)

    def column(i):
        same = tuple((z, z) for z in range(4))
        blocks(4 * i, 4 * i, 0, same + ((0, 1), (1, 2), (2, 3)), same)

    loop(6, own_pair)
    finish_round(0)
    send_round(1)
    for j in range(4):
        wait_recv(halo(j))
    loop(REMOTE, lambda i: prepare(BOXES + i, False))
    loop(4, tx_pair)
    reply(0).start()
    finish_round(1)
    send_round(2)
    loop(4, ty_pair)
    reply(1).start()
    loop(2, corner_pair)
    reply(2).start()
    reply(3).start()
    finish_round(2)
    loop(4, column)
    for i in range(5):
        gram_out[8 + i] = jnp.concatenate([grams[2 * i], grams[2 * i + 1]], axis=1)
    for j in range(4):
        wait_recv(reply(j))
    for i in range(BOXES):
        value = acc[i]
        for dy, dx, start, count, at_row in HALO:
            if start <= i < start + count:
                value = value + back[at_row + i - start]
        near_out[i] = value
    for j in range(4):
        wait_send(halo(j))
        wait_send(reply(j))
    for r in range(3):
        for q in range(1, 8):
            wait_send(exchange(r, q))


def factor_pairs(x, pairs):
    lane = lax.broadcasted_iota(jnp.int32, (8, 128), 1)
    sub = lax.broadcasted_iota(jnp.int32, (8, 128), 0)
    half = lane - lane % RANK
    spread = lambda v: jnp.broadcast_to(v, (8, 128))
    for j in range(0, RANK, 2):
        top = j // 8
        i0, i1 = half + j, half + j + 1
        pick = lambda v, idx: jnp.take_along_axis(v, idx, axis=1)
        for p in pairs:
            r0, r1 = spread(x[p, j : j + 1, :]), spread(x[p, j + 1 : j + 2, :])
            a, b, c = pick(r0, i0), pick(r0, i1), pick(r1, i1)
            sa = lax.rsqrt(a)
            out0 = r0 * sa
            inv = sa * sa
            t = b * inv
            sc = lax.rsqrt(c - b * t)
            out1 = (r1 - t * r0) * sc
            q1 = out1 * sc
            q0 = r0 * inv - t * q1
            for v in range(top, 8):
                old = x[p, 8 * v : 8 * v + 8, :]
                new = old - pick(old, i0) * q0 - pick(old, i1) * q1
                if v == top:
                    at = j - 8 * top
                    new = jnp.where(sub < at, old, jnp.where(sub == at, out0, jnp.where(sub == at + 1, out1, new)))
                x[p, 8 * v : 8 * v + 8, :] = new


def factor_kernel(near, gram, near_out, leaf_out, anc_out, x):
    for i, k in enumerate(BOX_AT):
        near_out[0, 0, :, k * PTS : (k + 1) * PTS] = near[i]
    x[...] = gram[...]
    factor_pairs(x, range(13))
    r = lax.broadcasted_iota(jnp.int32, (RANK, RANK), 0)
    c = lax.broadcasted_iota(jnp.int32, (RANK, RANK), 1)
    for p in range(13):
        for h in range(2):
            m = jnp.where(c >= r, x[p, :, RANK * h : RANK * (h + 1)], 0.0)
            if p < 8:
                leaf_out[0, 0, 2 * p + h] = m
            else:
                anc_out[0, 0, 2 * (p - 8) + h] = m


def vmem():
    return pl.BlockSpec(memory_space=pltpu.VMEM)


def on_device(sizes, comm, points, probes, near_boxes, leaf_bases, box_transfer, upper_transfer):
    near, gram = pl.pallas_call(
        functools.partial(main_kernel, sizes, comm),
        out_shape=(
            jax.ShapeDtypeStruct((BOXES, 8, PTS), F32),
            jax.ShapeDtypeStruct((13, RANK, 128), F32),
        ),
        in_specs=[vmem()] * 6,
        out_specs=(vmem(), vmem()),
        scratch_shapes=[
            pltpu.VMEM((BOXES + REMOTE, 16, PTS), F32),
            pltpu.VMEM((BOXES, PTS, 48), BF16),
            pltpu.VMEM((BOXES + REMOTE, 48, PTS), BF16),
            pltpu.VMEM((BOXES + REMOTE, 32, 128), F32),
            pltpu.VMEM((BOXES + REMOTE, 8, PTS), F32),
            pltpu.VMEM((REMOTE, 8, PTS), F32),
            pltpu.VMEM((10, PTS, PTS), BF16),
            pltpu.VMEM((10, RANK, RANK), F32),
            pltpu.VMEM((3, 3, 32, 128), F32),
            pltpu.VMEM((3, 7, 3, 32, 128), F32),
            pltpu.SemaphoreType.DMA((4,)),
            pltpu.SemaphoreType.DMA((4,)),
            pltpu.SemaphoreType.DMA((4,)),
            pltpu.SemaphoreType.DMA((4,)),
            pltpu.SemaphoreType.DMA((21,)),
            pltpu.SemaphoreType.DMA((21,)),
        ],
        compiler_params=pltpu.CompilerParams(
            collective_id=0 if comm else None, has_side_effects=True, vmem_limit_bytes=48 * 2**20
        ),
        name="near_and_grams",
    )(points, probes, near_boxes, leaf_bases, box_transfer, upper_transfer)
    return pl.pallas_call(
        factor_kernel,
        out_shape=(
            jax.ShapeDtypeStruct((1, 1, 8, BOXES * PTS), F32),
            jax.ShapeDtypeStruct((1, 1, BOXES, RANK, RANK), F32),
            jax.ShapeDtypeStruct((1, 1, 10, RANK, RANK), F32),
        ),
        in_specs=[vmem()] * 2,
        out_specs=(vmem(),) * 3,
        scratch_shapes=[pltpu.VMEM((13, RANK, 128), F32)],
        compiler_params=pltpu.CompilerParams(vmem_limit_bytes=32 * 2**20),
        name="factors",
    )(near, gram)


def solution(mesh):
    return jax.shard_map(
        functools.partial(on_device, (mesh.shape["ty"], mesh.shape["tx"]), True),
        mesh=mesh,
        in_specs=(
            P("ty", "tx", None, None),
            P("ty", "tx", None, None),
            P("ty", "tx", None, None),
            P("ty", "tx", None, None),
            P("ty", "tx", None, None, None),
            P(),
        ),
        out_specs=(
            P("ty", "tx", None, None),
            P("ty", "tx", None, None, None),
            P("ty", "tx", None, None, None),
        ),
        check_vma=False,
    )
```

time: 394 us -> 67.6 us (0.17)
  the two profiles are of different devices: /device:TPU:6 before, /device:TPU:1 now
where the time goes in v1:
time: 67.6 us; the launch traced here: 67.3 us
  Pallas kernels  61.5 us (91%)
  local copies, waits for them, and re-layouts  5.07 us (8%)
    pallas_call x1, Pallas kernels, on_device(): pl.pallas_call(functools.partial(main_kernel, sizes, comm), out_shape=(ja...  51.6 us
    pallas_call x1, Pallas kernels, on_device(): pl.pallas_call(factor_kernel, out_shape=(jax.ShapeDtypeStruct((1, 1, 8, B...  9.91 us
    unnamed x11, local copies, waits for them, and re-layouts  5.07 us

profile of v1, /device:TPU:1, one launch (start us, length us, event | category | flops | bytes accessed | tf_op | source)
XLA Modules:
  0.0 67.3 jit_solution(9125317799398860776)
XLA Ops:
  0.6 0.0 copy-start.4
  0.6 0.8 %copy.9.pts = f32[1,1,3,4096]{3,2,1,0:T(4,128)S(1)} copy(f32[1,1,3,4096]{3,1,2,0:T(1,128)} %param.6) | data formatting | bytes 98304 | tf_op args[0]
  1.5 0.0 copy-done.4
  1.5 0.0 copy-start
  1.5 1.2 %copy-done = f32[1,1,64,4096]{3,2,1,0:T(8,128)S(1)} copy-done((f32[1,1,64,4096]{3,2,1,0:T(8,128)S(1)}, f32[1,1,64,4096]{3,2,1,0:T(8,128)}, u32[]{:S(2)}) %copy-start) | copy-done | bytes 1048600
  2.7 0.0 copy-start.1
  2.7 1.1 %copy-done.1 = f32[9,2,64,64]{3,2,1,0:T(8,128)S(1)} copy-done((f32[9,2,64,64]{3,2,1,0:T(8,128)S(1)}, f32[9,2,64,64]{3,2,1,0:T(8,128)}, u32[]{:S(2)}) %copy-start.1) | copy-done | bytes 294936
  3.8 0.0 copy-start.2
  3.8 1.0 %copy-done.2 = f32[1,1,16,64,64]{4,3,2,1,0:T(8,128)S(1)} copy-done((f32[1,1,16,64,64]{4,3,2,1,0:T(8,128)S(1)}, f32[1,1,16,64,64]{4,3,2,1,0:T(8,128)}, u32[]{:S(2)}) %copy-start.2) | copy-done | bytes 262168
  4.8 0.0 copy-start.3
  4.8 0.9 %copy-done.3 = f32[1,1,8,4096]{3,2,1,0:T(8,128)S(1)} copy-done((f32[1,1,8,4096]{3,2,1,0:T(8,128)S(1)}, f32[1,1,8,4096]{3,2,1,0:T(8,128)}, u32[]{:S(2)}) %copy-start.3) | copy-done | bytes 131096
  5.7 51.6 %near_and_grams.1 = (f32[16,8,256]{2,1,0:T(8,128)S(1)}, f32[13,64,128]{2,1,0:T(8,128)S(1)}) custom-call(f32[1,1,3,4096]{3,2,1,0:T(4,128)S(1)} %copy.9.pts, f32[1,1,8,4096]{3,2,1,0:T(8,128)S(1)} %copy-done.3, s32[1,1,16,27]{3,2,1,0:T(8,128)S(1)} %copy-done.4, f32[1,1,64,4096]{3,2,1,0:T(8,128)S(1)} %copy-done, f32[1,1,16,64,64]{4,3,2,1,0:T(8,128)S(1)} %copy-done.2, ...), custom_call_target="tpu_custom_call" | custom-call | tf_op jit(solution)/shard_map/near_and_grams/pallas_call | solution.py:357
  57.4 9.9 %factors.1 = (f32[1,1,8,4096]{3,2,1,0:T(8,128)}, f32[1,1,16,64,64]{4,3,2,1,0:T(8,128)}, f32[1,1,10,64,64]{4,3,2,1,0:T(8,128)}) custom-call(f32[16,8,256]{2,1,0:T(8,128)S(1)} %get-tuple-element.5.near, f32[13,64,128]{2,1,0:T(8,128)S(1)} %get-tuple-element.6.gram), custom_call_target="tpu_custom_call" | custom-call | tf_op jit(solution)/shard_map/factors/pallas_call | solution.py:388
Async XLA Ops:
  0.6 0.9 %copy-start.4 = (s32[1,1,16,27]{3,2,1,0:T(8,128)S(1)}, s32[1,1,16,27]{3,2,1,0:T(8,128)}, u32[]{:S(2)}) copy-start(s32[1,1,16,27]{3,2,1,0:T(8,128)} %near.1) | copy-start | bytes 5188
  1.5 1.2 %copy-start = (f32[1,1,64,4096]{3,2,1,0:T(8,128)S(1)}, f32[1,1,64,4096]{3,2,1,0:T(8,128)}, u32[]{:S(2)}) copy-start(f32[1,1,64,4096]{3,2,1,0:T(8,128)} %leaf.1) | copy-start | bytes 3145732
  2.7 1.1 %copy-start.1 = (f32[9,2,64,64]{3,2,1,0:T(8,128)S(1)}, f32[9,2,64,64]{3,2,1,0:T(8,128)}, u32[]{:S(2)}) copy-start(f32[9,2,64,64]{3,2,1,0:T(8,128)} %upper.1) | copy-start | bytes 884740
  3.8 1.0 %copy-start.2 = (f32[1,1,16,64,64]{4,3,2,1,0:T(8,128)S(1)}, f32[1,1,16,64,64]{4,3,2,1,0:T(8,128)}, u32[]{:S(2)}) copy-start(f32[1,1,16,64,64]{4,3,2,1,0:T(8,128)} %trans.1) | copy-start | bytes 786436
  4.8 0.9 %copy-start.3 = (f32[1,1,8,4096]{3,2,1,0:T(8,128)S(1)}, f32[1,1,8,4096]{3,2,1,0:T(8,128)}, u32[]{:S(2)}) copy-start(f32[1,1,8,4096]{3,2,1,0:T(8,128)} %prb.1) | copy-start | bytes 393220

commit v2 on v1

--- a/solution.py
+++ b/solution.py
@@ -11,8 +11,8 @@
 MESH = pl.DeviceIdType.MESH
 HIGHEST = lax.Precision.HIGHEST
 F32, BF16 = jnp.float32, jnp.bfloat16
-LN2 = math.log(2.0)
-ALPHA = math.sqrt(3.0) / LN2
+LOG2E = 1.0 / math.log(2.0)
+ALPHA = math.sqrt(3.0)
 BOXES, PTS, RANK = 16, 256, 64
 COLUMNS = ((0, 1), (0, 0), (1, 0), (1, 1))
 BOX_AT = tuple(x + 2 * y + 4 * z for x, y in COLUMNS for z in range(4))
@@ -56,8 +56,8 @@
 
 def matern(square):
     s = jnp.maximum(square, 1e-12)
-    u = s * lax.rsqrt(s)
-    return ((1.0 + LN2 * u) * jnp.exp2(-u)).astype(BF16)
+    c = s * lax.rsqrt(s)
+    return ((1.0 + c) * jnp.exp2(c * -LOG2E)).astype(BF16)
 
 
 def halves(packed):
@@ -76,9 +76,21 @@
     return None
 
 
-def main_kernel(sizes, comm, pts, prb, near, leaf, trans, upper, near_out, gram_out,
-                box, left, right, mask, acc, back, kern, grams, tree_out, tree_in,
+def main_kernel(sizes, comm, pts_in, prb_in, near_in, leaf_in, trans_in, upper_in,
+                near_out, leaf_out, gram_out,
+                pts, prb, near, leaf, trans, upper, loaded,
+                box, left, right, mask, acc, back, kern, grams, paths, tree_out, tree_in,
+                x0, x1, x2, x3, x4, x5, x6, x7,
                 halo_send, halo_recv, back_send, back_recv, tree_send, tree_recv):
+    xs = (x0, x1, x2, x3, x4, x5, x6, x7)
+    loads = [
+        pltpu.make_async_copy(src, dst, loaded.at[i])
+        for i, (src, dst) in enumerate((
+            (pts_in, pts), (prb_in.at[0, 0], prb), (near_in.at[0, 0], near),
+            (leaf_in.at[0, 0], leaf), (trans_in.at[0, 0], trans), (upper_in, upper)))
+    ]
+    for load in loads:
+        load.start()
     n_ty, n_tx = sizes
     ty, tx = (lax.axis_index("ty"), lax.axis_index("tx")) if comm else (jnp.int32(0), jnp.int32(0))
     center = ((2 * ty + 1).astype(F32), (2 * tx + 1).astype(F32))
@@ -106,12 +118,16 @@
         for peer in peers:
             pl.semaphore_signal(barrier, inc=1, device_id=peer, device_id_type=MESH)
 
+    for load in loads[:3]:
+        load.wait()
     for i, k in enumerate(BOX_AT):
         cols = slice(k * PTS, (k + 1) * PTS)
-        box[i, 0:3, :] = pts[0, 0, :, cols]
-        box[i, 8:16, :] = prb[0, 0, :, cols]
+        for c in range(3):
+            for h in range(2):
+                box[i, c : c + 1, 128 * h : 128 * h + 128] = pts[c, 2 * k + h : 2 * k + h + 1, :]
+        box[i, 8:16, :] = prb[:, cols]
         box[i, 3:8, :] = jnp.zeros((5, PTS), F32)
-        box[i, 3:4, 0:27] = jnp.where(near[0, 0, k : k + 1, :] >= 0, 1.0, 0.0)
+        box[i, 3:4, 0:27] = jnp.where(near[k : k + 1, :] >= 0, 1.0, 0.0)
 
     if comm:
         pl.semaphore_wait(barrier, len(peers))
@@ -157,28 +173,34 @@
     for j in range(4):
         halo(j).start()
 
+    for load in loads[3:]:
+        load.wait()
+    for r in range(3):
+        path = None
+        for i in range(3):
+            step = upper[3 * r + i, bits[3 * r + i]]
+            path = step if path is None else dot(path, step, 1, 0, HIGHEST)
+            paths[3 * r + i] = path
     total = jnp.zeros((RANK, RANK), F32)
     pair = []
     for k in range(BOXES):
-        v = leaf[0, 0, :, k * PTS : (k + 1) * PTS]
+        v = leaf[:, k * PTS : (k + 1) * PTS]
         stack = jnp.concatenate(split3(v), axis=0).astype(BF16)
         c = dot(stack, stack, 1, 1)
         g = c[128:, :64] + c[:64, 128:] + c[64:128, 64:128]
         g = g + (c[:64, 64:128] + c[64:128, :64]) + c[:64, :64]
         pair.append(g)
         if k % 2:
-            gram_out[k // 2] = jnp.concatenate(pair, axis=1)
+            xs[k // 2][...] = jnp.concatenate(pair, axis=1)
             pair = []
-        t = trans[0, 0, k]
+        t = trans[k]
         total = total + dot(t, dot(g, t, 1, 0, HIGHEST), 0, 0, HIGHEST)
     grams[0] = total
 
     def send_round(r):
         node = grams[3 * r]
-        path = None
         for i in range(3):
-            step = upper[3 * r + i, bits[3 * r + i]]
-            path = step if path is None else dot(path, step, 1, 0, HIGHEST)
+            path = paths[3 * r + i]
             term = dot(path, dot(node, path, 1, 0, HIGHEST), 0, 0, HIGHEST)
             tree_out[r, 2 - i] = packed(term)
         for q in range(1, 8):
@@ -210,24 +232,28 @@
         mask[i] = dot(slots, ones, 1, 0)
         acc[i] = jnp.zeros((8, PTS), F32)
 
-    def loop(n, body):
-        lax.fori_loop(0, n, lambda i, c: (body(i), c)[1], 0)
+    def loop(n, body, unroll=2):
+        lax.fori_loop(0, n, lambda i, c: (body(i), c)[1], 0, unroll=unroll)
 
     def probe(i, owner, slot):
         m = mask[owner, pl.ds(slot, 1), :]
         return (box[i, 8:16, :] * jnp.concatenate([m, m], axis=1)).astype(BF16)
 
-    def blocks(a0, b0, step, pairs, one_sided=()):
+    def factor(t):
+        for p in range(8):
+            factor_step(xs[p], leaf_out, p, 2 * t)
+
+    def blocks(a0, b0, step, pairs, one_sided=(), steps=(), base=0):
         sums = {}
 
         def first(m, za, zb):
-            kern[m] = matern(dot(left[a0 + za], right[b0 + zb], 1, 0))
+            kern[base + m] = matern(dot(left[a0 + za], right[b0 + zb], 1, 0))
 
         def add(key, value):
             sums[key] = value if key not in sums else sums[key] + value
 
         def second(m, za, zb):
-            block = kern[m]
+            block = kern[base + m]
             a, b = a0 + za, b0 + zb
             slot = 13 + step + (zb - za)
             add(("a", za), dot(probe(b, a, slot), block, 1, 1))
@@ -236,6 +262,8 @@
 
         late = 2
         for m in range(len(pairs) + late):
+            if m % 5 == 1 and m // 5 < len(steps):
+                factor(steps[m // 5])
             if m < len(pairs):
                 first(m, *pairs[m])
             if m >= late:
@@ -244,50 +272,50 @@
             at_box = (a0 if side == "a" else b0) + z
             acc[at_box] = acc[at_box] + value
 
-    loop(BOXES, lambda i: prepare(i, True))
-
-    def own_pair(i):
+    loop(BOXES, lambda i: prepare(i, True), 4)
+
+    def own_pair(i, base=0):
         d, j = i // 2 + 1, lax.rem(i, 2)
         a = j * (1 + 1 // d)
         b = a + d - 2 * a * (d // 3)
         x = lambda p: p // 2
         y = lambda p: 1 - lax.rem((p + 1) // 2, 2)
-        blocks(4 * a, 4 * b, 9 * (x(b) - x(a)) + 3 * (y(b) - y(a)), Z_PAIRS)
-
-    def tx_pair(i):
+        blocks(4 * a, 4 * b, 9 * (x(b) - x(a)) + 3 * (y(b) - y(a)), Z_PAIRS, base=base, steps=(0 + 2 * i, 1 + 2 * i))
+
+    def tx_pair(i, base=0):
         xa, xb = lax.rem(i, 2), i // 2
-        blocks(12 * xa, BOXES + 4 * xb, 9 * (xb - xa) + 3, Z_PAIRS)
-
-    def ty_pair(i):
+        blocks(12 * xa, BOXES + 4 * xb, 9 * (xb - xa) + 3, Z_PAIRS, base=base, steps=(12 + 2 * i, 13 + 2 * i))
+
+    def ty_pair(i, base=0):
         ya, p = lax.rem(i, 2), i // 2
-        blocks(8 + 4 * ya, BOXES + 8 + 4 * p, 9 + 3 * (1 - p - ya), Z_PAIRS)
-
-    def corner_pair(i):
-        blocks(12 - 4 * i, BOXES + 16 + 4 * i, 9 + 3 * (1 - 2 * i), Z_PAIRS)
-
-    def column(i):
+        blocks(8 + 4 * ya, BOXES + 8 + 4 * p, 9 + 3 * (1 - p - ya), Z_PAIRS, base=base, steps=(20 + 2 * i, 21 + 2 * i))
+
+    def corner_pair(i, base=0):
+        blocks(12 - 4 * i, BOXES + 16 + 4 * i, 9 + 3 * (1 - 2 * i), Z_PAIRS, base=base, steps=(28 + 2 * i, 29 + 2 * i))
+
+    def column(i, base=0):
         same = tuple((z, z) for z in range(4))
-        blocks(4 * i, 4 * i, 0, same + ((0, 1), (1, 2), (2, 3)), same)
-
-    loop(6, own_pair)
+        blocks(4 * i, 4 * i, 0, same + ((0, 1), (1, 2), (2, 3)), same, base=base)
+
+    loop(3, lambda i: (own_pair(2 * i), own_pair(2 * i + 1, 10)), 1)
     finish_round(0)
     send_round(1)
     for j in range(4):
         wait_recv(halo(j))
-    loop(REMOTE, lambda i: prepare(BOXES + i, False))
-    loop(4, tx_pair)
+    loop(REMOTE, lambda i: prepare(BOXES + i, False), 4)
+    loop(2, lambda i: (tx_pair(2 * i), tx_pair(2 * i + 1, 10)), 1)
     reply(0).start()
     finish_round(1)
     send_round(2)
-    loop(4, ty_pair)
+    loop(2, lambda i: (ty_pair(2 * i), ty_pair(2 * i + 1, 10)), 1)
     reply(1).start()
-    loop(2, corner_pair)
+    loop(1, lambda i: (corner_pair(2 * i), corner_pair(2 * i + 1, 10)), 1)
     reply(2).start()
     reply(3).start()
     finish_round(2)
-    loop(4, column)
+    loop(2, lambda i: (column(2 * i), column(2 * i + 1, 10)), 1)
     for i in range(5):
-        gram_out[8 + i] = jnp.concatenate([grams[2 * i], grams[2 * i + 1]], axis=1)
+        gram_out[i] = jnp.concatenate([grams[2 * i], grams[2 * i + 1]], axis=1)
     for j in range(4):
         wait_recv(reply(j))
     for i in range(BOXES):
@@ -304,49 +332,55 @@
             wait_send(exchange(r, q))
 
 
-def factor_pairs(x, pairs):
+def factor_step(x, out, p, j, top=0):
     lane = lax.broadcasted_iota(jnp.int32, (8, 128), 1)
-    sub = lax.broadcasted_iota(jnp.int32, (8, 128), 0)
     half = lane - lane % RANK
-    spread = lambda v: jnp.broadcast_to(v, (8, 128))
-    for j in range(0, RANK, 2):
-        top = j // 8
-        i0, i1 = half + j, half + j + 1
-        pick = lambda v, idx: jnp.take_along_axis(v, idx, axis=1)
-        for p in pairs:
-            r0, r1 = spread(x[p, j : j + 1, :]), spread(x[p, j + 1 : j + 2, :])
-            a, b, c = pick(r0, i0), pick(r0, i1), pick(r1, i1)
-            sa = lax.rsqrt(a)
-            out0 = r0 * sa
-            inv = sa * sa
-            t = b * inv
-            sc = lax.rsqrt(c - b * t)
-            out1 = (r1 - t * r0) * sc
-            q1 = out1 * sc
-            q0 = r0 * inv - t * q1
-            for v in range(top, 8):
-                old = x[p, 8 * v : 8 * v + 8, :]
-                new = old - pick(old, i0) * q0 - pick(old, i1) * q1
-                if v == top:
-                    at = j - 8 * top
-                    new = jnp.where(sub < at, old, jnp.where(sub == at, out0, jnp.where(sub == at + 1, out1, new)))
-                x[p, 8 * v : 8 * v + 8, :] = new
-
-
-def factor_kernel(near, gram, near_out, leaf_out, anc_out, x):
+    i0, i1 = half + j, half + j + 1
+    pick = lambda v, idx: jnp.take_along_axis(v, idx, axis=1)
+    r0 = jnp.broadcast_to(x[pl.ds(j, 1), :], (8, 128))
+    r1 = jnp.broadcast_to(x[pl.ds(j + 1, 1), :], (8, 128))
+    a, b, c = pick(r0, i0), pick(r0, i1), pick(r1, i1)
+    sa = lax.rsqrt(a)
+    inv = sa * sa
+    t = b * inv
+    sc = lax.rsqrt(c - b * t)
+    out0, out1 = r0 * sa, (r1 - t * r0) * sc
+    out[p, pl.ds(j, 1), :] = out0[0:1]
+    out[p, pl.ds(j + 1, 1), :] = out1[0:1]
+    q1 = out1 * sc
+    q0 = r0 * inv - t * q1
+    for v in range(top, 8):
+        rows = slice(8 * v, 8 * v + 8)
+        old = x[rows, :]
+        x[rows, :] = old - pick(old, i0) * q0 - pick(old, i1) * q1
+
+
+def factor_kernel(near, leaf_in, gram_in, near_out, leaf_out, anc_out, leaf, gram, done, x0, x1, x2, x3, x4, sems):
+    xs = (x0, x1, x2, x3, x4)
+    copies = [pltpu.make_async_copy(gram_in, gram, sems.at[16]), pltpu.make_async_copy(leaf_in, leaf, sems.at[17])]
     for i, k in enumerate(BOX_AT):
-        near_out[0, 0, :, k * PTS : (k + 1) * PTS] = near[i]
-    x[...] = gram[...]
-    factor_pairs(x, range(13))
+        cols = pl.ds(k * PTS, PTS)
+        copies.append(pltpu.make_async_copy(near.at[i], near_out.at[0, 0, :, cols], sems.at[i]))
+    for copy in copies:
+        copy.start()
+    copies[0].wait()
+    for p, x in enumerate(xs):
+        x[...] = gram[p]
     r = lax.broadcasted_iota(jnp.int32, (RANK, RANK), 0)
     c = lax.broadcasted_iota(jnp.int32, (RANK, RANK), 1)
-    for p in range(13):
+    triangle = lambda m, h: jnp.where(c >= r, m[:, RANK * h : RANK * (h + 1)], 0.0)
+    copies[1].wait()
+    for p in range(8):
         for h in range(2):
-            m = jnp.where(c >= r, x[p, :, RANK * h : RANK * (h + 1)], 0.0)
-            if p < 8:
-                leaf_out[0, 0, 2 * p + h] = m
-            else:
-                anc_out[0, 0, 2 * (p - 8) + h] = m
+            leaf_out[0, 0, 2 * p + h] = triangle(leaf[p], h)
+    for j in range(0, RANK, 2):
+        for p, x in enumerate(xs):
+            factor_step(x, done, p, j, j // 8)
+    for p in range(5):
+        for h in range(2):
+            anc_out[0, 0, 2 * p + h] = triangle(done[p], h)
+    for copy in copies[2:]:
+        copy.wait()
 
 
 def vmem():
@@ -354,25 +388,35 @@
 
 
 def on_device(sizes, comm, points, probes, near_boxes, leaf_bases, box_transfer, upper_transfer):
-    near, gram = pl.pallas_call(
+    near, leaf, gram = pl.pallas_call(
         functools.partial(main_kernel, sizes, comm),
         out_shape=(
             jax.ShapeDtypeStruct((BOXES, 8, PTS), F32),
-            jax.ShapeDtypeStruct((13, RANK, 128), F32),
+            jax.ShapeDtypeStruct((8, RANK, 128), F32),
+            jax.ShapeDtypeStruct((5, RANK, 128), F32),
         ),
-        in_specs=[vmem()] * 6,
-        out_specs=(vmem(), vmem()),
+        in_specs=[pl.BlockSpec(memory_space=pl.ANY)] * 6,
+        out_specs=(vmem(),) * 3,
         scratch_shapes=[
+            pltpu.VMEM((3, 32, 128), F32),
+            pltpu.VMEM((8, BOXES * PTS), F32),
+            pltpu.VMEM((BOXES, 27), jnp.int32),
+            pltpu.VMEM((RANK, BOXES * PTS), F32),
+            pltpu.VMEM((BOXES, RANK, RANK), F32),
+            pltpu.VMEM((9, 2, RANK, RANK), F32),
+            pltpu.SemaphoreType.DMA((6,)),
             pltpu.VMEM((BOXES + REMOTE, 16, PTS), F32),
             pltpu.VMEM((BOXES, PTS, 48), BF16),
             pltpu.VMEM((BOXES + REMOTE, 48, PTS), BF16),
             pltpu.VMEM((BOXES + REMOTE, 32, 128), F32),
             pltpu.VMEM((BOXES + REMOTE, 8, PTS), F32),
             pltpu.VMEM((REMOTE, 8, PTS), F32),
-            pltpu.VMEM((10, PTS, PTS), BF16),
+            pltpu.VMEM((20, PTS, PTS), BF16),
             pltpu.VMEM((10, RANK, RANK), F32),
+            pltpu.VMEM((9, RANK, RANK), F32),
             pltpu.VMEM((3, 3, 32, 128), F32),
             pltpu.VMEM((3, 7, 3, 32, 128), F32),
+            *[pltpu.VMEM((RANK, 128), F32)] * 8,
             pltpu.SemaphoreType.DMA((4,)),
             pltpu.SemaphoreType.DMA((4,)),
             pltpu.SemaphoreType.DMA((4,)),
@@ -381,10 +425,10 @@
             pltpu.SemaphoreType.DMA((21,)),
         ],
         compiler_params=pltpu.CompilerParams(
-            collective_id=0 if comm else None, has_side_effects=True, vmem_limit_bytes=48 * 2**20
+            collective_id=0 if comm else None, has_side_effects=True, vmem_limit_bytes=62 * 2**20
         ),
         name="near_and_grams",
-    )(points, probes, near_boxes, leaf_bases, box_transfer, upper_transfer)
+    )(points.reshape(3, 32, 128), probes, near_boxes, leaf_bases, box_transfer, upper_transfer)
     return pl.pallas_call(
         factor_kernel,
         out_shape=(
@@ -392,12 +436,18 @@
             jax.ShapeDtypeStruct((1, 1, BOXES, RANK, RANK), F32),
             jax.ShapeDtypeStruct((1, 1, 10, RANK, RANK), F32),
         ),
-        in_specs=[vmem()] * 2,
-        out_specs=(vmem(),) * 3,
-        scratch_shapes=[pltpu.VMEM((13, RANK, 128), F32)],
-        compiler_params=pltpu.CompilerParams(vmem_limit_bytes=32 * 2**20),
+        in_specs=[pl.BlockSpec(memory_space=pl.ANY)] * 3,
+        out_specs=(pl.BlockSpec(memory_space=pl.ANY), vmem(), vmem()),
+        scratch_shapes=[
+            pltpu.VMEM((8, RANK, 128), F32),
+            pltpu.VMEM((5, RANK, 128), F32),
+            pltpu.VMEM((5, RANK, 128), F32),
+            *[pltpu.VMEM((RANK, 128), F32)] * 5,
+            pltpu.SemaphoreType.DMA((18,)),
+        ],
+        compiler_params=pltpu.CompilerParams(vmem_limit_bytes=62 * 2**20),
         name="factors",
-    )(near, gram)
+    )(near, leaf, gram)
 
 
 def solution(mesh):

time: 67.6 us -> 54.4 us (0.80)
  Pallas kernels: 61.5 us -> 53.4 us
  local copies, waits for them, and re-layouts: 5.07 us -> 0 us
    unnamed x11 -> x0, local copies, waits for them, and re-layouts: 5.07 us -> none
    pallas_call x1, Pallas kernels: 51.6 us -> 46.9 us  [on_device(): pl.pallas_call(functools.partial(main_kernel, sizes, comm), out_shape=(ja...]
    pallas_call x1, Pallas kernels: 9.91 us -> 6.5 us  [on_device(): pl.pallas_call(factor_kernel, out_shape=(jax.ShapeDtypeStruct((1, 1, 8, B...]
where the time goes in v2:
time: 54.4 us; the launch traced here: 54.2 us
  Pallas kernels  53.4 us (98%)
  between operations  0.82 us (2%)
    pallas_call x1, Pallas kernels, on_device(): pl.pallas_call(functools.partial(main_kernel, sizes, comm), out_shape=(ja...  46.9 us
    pallas_call x1, Pallas kernels, on_device(): pl.pallas_call(factor_kernel, out_shape=(jax.ShapeDtypeStruct((1, 1, 8, B...  6.5 us

profile of v2, /device:TPU:1, one launch (start us, length us, event | category | flops | bytes accessed | tf_op | source)
XLA Modules:
  0.0 54.2 jit_solution(13252414737024189178)
XLA Ops:
  0.6 46.9 %near_and_grams.1 = (f32[16,8,256]{2,1,0:T(8,128)}, f32[8,64,128]{2,1,0:T(8,128)}, f32[5,64,128]{2,1,0:T(8,128)}) custom-call(f32[3,32,128]{2,1,0:T(8,128)} %bitcast.1, f32[1,1,8,4096]{3,2,1,0:T(8,128)} %prb_in.1, s32[1,1,16,27]{3,2,1,0:T(8,128)} %near_in.1, f32[1,1,64,4096]{3,2,1,0:T(8,128)} %leaf_in.1, f32[1,1,16,64,64]{4,3,2,1,0:T(8,128)} %trans_in.1, ...), custom_call_target="tpu_custom_call" | custom-call | tf_op jit(solution)/shard_map/near_and_grams/pallas_call | solution.py:391
  47.5 6.5 %factors.1 = (f32[1,1,8,4096]{3,2,1,0:T(8,128)}, f32[1,1,16,64,64]{4,3,2,1,0:T(8,128)}, f32[1,1,10,64,64]{4,3,2,1,0:T(8,128)}) custom-call(f32[16,8,256]{2,1,0:T(8,128)} %get-tuple-element.6.near, f32[8,64,128]{2,1,0:T(8,128)} %get-tuple-element.7.leaf_in, f32[5,64,128]{2,1,0:T(8,128)} %get-tuple-element.8.gram_in), custom_call_target="tpu_custom_call" | custom-call | tf_op jit(solution)/shard_map/factors/pallas_call | solution.py:432

commit v3 on v2

--- a/solution.py
+++ b/solution.py
@@ -14,6 +14,7 @@
 LOG2E = 1.0 / math.log(2.0)
 ALPHA = math.sqrt(3.0)
 BOXES, PTS, RANK = 16, 256, 64
+TEST_TY = 6
 COLUMNS = ((0, 1), (0, 0), (1, 0), (1, 1))
 BOX_AT = tuple(x + 2 * y + 4 * z for x, y in COLUMNS for z in range(4))
 HALO = ((0, -1, 4, 8, 0), (-1, 0, 0, 8, 8), (-1, -1, 4, 4, 16), (-1, 1, 0, 4, 20))
@@ -92,7 +93,7 @@
     for load in loads:
         load.start()
     n_ty, n_tx = sizes
-    ty, tx = (lax.axis_index("ty"), lax.axis_index("tx")) if comm else (jnp.int32(0), jnp.int32(0))
+    ty, tx = (lax.axis_index("ty"), lax.axis_index("tx")) if comm else (jnp.int32(TEST_TY), jnp.int32(0))
     center = ((2 * ty + 1).astype(F32), (2 * tx + 1).astype(F32))
 
     def at(dy, dx):
@@ -118,6 +119,20 @@
         for peer in peers:
             pl.semaphore_signal(barrier, inc=1, device_id=peer, device_id_type=MESH)
 
+    z = ty // 2 + 3 * (1 - (ty * n_tx + tx + n_ty * n_tx - 1) // (n_ty * n_tx))
+    near_z, first_z = 1 - z // 4, 1 - (z + 7) // 8
+    pairs_ahead = near_z * (4 - z) - first_z
+    columns_ahead = near_z + first_z
+    columns_next = columns_ahead + 1 - near_z
+
+    @pl.when(ty == n_ty - 1)
+    def _():
+        box[24:40] = jnp.zeros((16, 16, PTS), F32)
+
+    @pl.when(ty == 0)
+    def _():
+        back[8:24] = jnp.zeros((16, 8, PTS), F32)
+
     for load in loads[:3]:
         load.wait()
     for i, k in enumerate(BOX_AT):
@@ -129,9 +144,6 @@
         box[i, 3:8, :] = jnp.zeros((5, PTS), F32)
         box[i, 3:4, 0:27] = jnp.where(near[k : k + 1, :] >= 0, 1.0, 0.0)
 
-    if comm:
-        pl.semaphore_wait(barrier, len(peers))
-
     def halo(j):
         dy, dx, first, count, row = HALO[j]
         src, dst = box.at[pl.ds(first, count)], box.at[pl.ds(BOXES + row, count)]
@@ -169,9 +181,6 @@
             copy.wait_recv()
         else:
             copy.wait()
-
-    for j in range(4):
-        halo(j).start()
 
     for load in loads[3:]:
         load.wait()
@@ -215,8 +224,6 @@
                 node = node + tree_in[r, q - 1, 2 - i]
             grams[3 * r + i + 1] = halves(node)
 
-    send_round(0)
-
     lane = lax.broadcasted_iota(jnp.int32, (32, 128), 1)
     row = lax.broadcasted_iota(jnp.int32, (32, 128), 0)
     ones = jnp.ones((128, 128), BF16)
@@ -232,8 +239,8 @@
         mask[i] = dot(slots, ones, 1, 0)
         acc[i] = jnp.zeros((8, PTS), F32)
 
-    def loop(n, body, unroll=2):
-        lax.fori_loop(0, n, lambda i, c: (body(i), c)[1], 0, unroll=unroll)
+    def loop(n, body, unroll=1, first=0):
+        lax.fori_loop(first, n, lambda i, c: (body(i), c)[1], 0, unroll=unroll)
 
     def probe(i, owner, slot):
         m = mask[owner, pl.ds(slot, 1), :]
@@ -274,59 +281,102 @@
 
     loop(BOXES, lambda i: prepare(i, True), 4)
 
-    def own_pair(i, base=0):
+    def own_pair(i, base, begin):
         d, j = i // 2 + 1, lax.rem(i, 2)
         a = j * (1 + 1 // d)
         b = a + d - 2 * a * (d // 3)
         x = lambda p: p // 2
         y = lambda p: 1 - lax.rem((p + 1) // 2, 2)
-        blocks(4 * a, 4 * b, 9 * (x(b) - x(a)) + 3 * (y(b) - y(a)), Z_PAIRS, base=base, steps=(0 + 2 * i, 1 + 2 * i))
+        blocks(4 * a, 4 * b, 9 * (x(b) - x(a)) + 3 * (y(b) - y(a)), Z_PAIRS, base=base, steps=(begin + 2 * i, begin + 1 + 2 * i))
 
     def tx_pair(i, base=0):
         xa, xb = lax.rem(i, 2), i // 2
-        blocks(12 * xa, BOXES + 4 * xb, 9 * (xb - xa) + 3, Z_PAIRS, base=base, steps=(12 + 2 * i, 13 + 2 * i))
+        blocks(12 * xa, BOXES + 4 * xb, 9 * (xb - xa) + 3, Z_PAIRS, base=base, steps=(done + 0 + 2 * i, done + 1 + 2 * i))
 
     def ty_pair(i, base=0):
         ya, p = lax.rem(i, 2), i // 2
-        blocks(8 + 4 * ya, BOXES + 8 + 4 * p, 9 + 3 * (1 - p - ya), Z_PAIRS, base=base, steps=(20 + 2 * i, 21 + 2 * i))
+        blocks(8 + 4 * ya, BOXES + 8 + 4 * p, 9 + 3 * (1 - p - ya), Z_PAIRS, base=base, steps=(done + 8 + 2 * i, done + 9 + 2 * i))
 
     def corner_pair(i, base=0):
-        blocks(12 - 4 * i, BOXES + 16 + 4 * i, 9 + 3 * (1 - 2 * i), Z_PAIRS, base=base, steps=(28 + 2 * i, 29 + 2 * i))
+        blocks(12 - 4 * i, BOXES + 16 + 4 * i, 9 + 3 * (1 - 2 * i), Z_PAIRS, base=base, steps=(done + 16 + 2 * i, done + 17 + 2 * i))
 
     def column(i, base=0):
         same = tuple((z, z) for z in range(4))
         blocks(4 * i, 4 * i, 0, same + ((0, 1), (1, 2), (2, 3)), same, base=base)
 
-    loop(3, lambda i: (own_pair(2 * i), own_pair(2 * i + 1, 10)), 1)
+    def own_pairs(first, last, begin):
+        loop(last, lambda i: (own_pair(2 * i, 0, begin), own_pair(2 * i + 1, 10, begin)), 1, first)
+
+    def columns(first, last):
+        loop(last, lambda i: (column(2 * i), column(2 * i + 1, 10)), 1, first)
+
+    own_pairs(0, pairs_ahead, 0)
+    columns(0, columns_ahead)
+    if comm:
+        pl.semaphore_wait(barrier, len(peers))
+    halo(0).start()
+
+    @pl.when(ty > 0)
+    def _():
+        for j in range(1, 4):
+            halo(j).start()
+
+    send_round(0)
+    columns(columns_ahead, columns_next)
     finish_round(0)
     send_round(1)
-    for j in range(4):
-        wait_recv(halo(j))
-    loop(REMOTE, lambda i: prepare(BOXES + i, False), 4)
-    loop(2, lambda i: (tx_pair(2 * i), tx_pair(2 * i + 1, 10)), 1)
-    reply(0).start()
+    columns(columns_next, 2)
     finish_round(1)
     send_round(2)
-    loop(2, lambda i: (ty_pair(2 * i), ty_pair(2 * i + 1, 10)), 1)
-    reply(1).start()
-    loop(1, lambda i: (corner_pair(2 * i), corner_pair(2 * i + 1, 10)), 1)
-    reply(2).start()
-    reply(3).start()
+    wait_recv(halo(0))
+
+    @pl.when(ty < n_ty - 1)
+    def _():
+        for j in range(1, 4):
+            wait_recv(halo(j))
+
+    loop(REMOTE, lambda i: prepare(BOXES + i, False), 4)
+    done = 4 * pairs_ahead
+    loop(2, lambda i: (tx_pair(2 * i), tx_pair(2 * i + 1, 10)))
+    reply(0).start()
+    loop(2, lambda i: (ty_pair(2 * i), ty_pair(2 * i + 1, 10)))
+    loop(1, lambda i: (corner_pair(2 * i), corner_pair(2 * i + 1, 10)))
+
+    @pl.when(ty < n_ty - 1)
+    def _():
+        for j in range(1, 4):
+            reply(j).start()
+
+    own_pairs(pairs_ahead, 3, 20)
     finish_round(2)
-    loop(2, lambda i: (column(2 * i), column(2 * i + 1, 10)), 1)
     for i in range(5):
         gram_out[i] = jnp.concatenate([grams[2 * i], grams[2 * i + 1]], axis=1)
-    for j in range(4):
-        wait_recv(reply(j))
+    wait_recv(reply(0))
+
+    @pl.when(ty > 0)
+    def _():
+        for j in range(1, 4):
+            wait_recv(reply(j))
+
     for i in range(BOXES):
         value = acc[i]
         for dy, dx, start, count, at_row in HALO:
             if start <= i < start + count:
                 value = value + back[at_row + i - start]
         near_out[i] = value
-    for j in range(4):
-        wait_send(halo(j))
-        wait_send(reply(j))
+    wait_send(halo(0))
+    wait_send(reply(0))
+
+    @pl.when(ty > 0)
+    def _():
+        for j in range(1, 4):
+            wait_send(halo(j))
+
+    @pl.when(ty < n_ty - 1)
+    def _():
+        for j in range(1, 4):
+            wait_send(reply(j))
+
     for r in range(3):
         for q in range(1, 8):
             wait_send(exchange(r, q))

time: 54.4 us -> 63.7 us (1.17)
  Pallas kernels: 53.4 us -> 62.7 us
    pallas_call x1, Pallas kernels: 46.9 us -> 56.2 us  [on_device(): pl.pallas_call(functools.partial(main_kernel, sizes, comm), out_shape=(ja...]
where the time goes in v3:
time: 63.7 us; the launch traced here: 63.5 us
  Pallas kernels  62.7 us (98%)
  between operations  0.82 us (1%)
    pallas_call x1, Pallas kernels, on_device(): pl.pallas_call(functools.partial(main_kernel, sizes, comm), out_shape=(ja...  56.2 us
    pallas_call x1, Pallas kernels, on_device(): pl.pallas_call(factor_kernel, out_shape=(jax.ShapeDtypeStruct((1, 1, 8, B...  6.5 us

profile of v3, /device:TPU:1, one launch (start us, length us, event | category | flops | bytes accessed | tf_op | source)
XLA Modules:
  0.0 63.5 jit_solution(12040327570339132024)
XLA Ops:
  0.6 56.2 %near_and_grams.1 = (f32[16,8,256]{2,1,0:T(8,128)}, f32[8,64,128]{2,1,0:T(8,128)}, f32[5,64,128]{2,1,0:T(8,128)}) custom-call(f32[3,32,128]{2,1,0:T(8,128)} %bitcast.1, f32[1,1,8,4096]{3,2,1,0:T(8,128)} %prb_in.1, s32[1,1,16,27]{3,2,1,0:T(8,128)} %near_in.1, f32[1,1,64,4096]{3,2,1,0:T(8,128)} %leaf_in.1, f32[1,1,16,64,64]{4,3,2,1,0:T(8,128)} %trans_in.1, ...), custom_call_target="tpu_custom_call" | custom-call | tf_op jit(solution)/shard_map/near_and_grams/pallas_call | solution.py:441
  56.8 6.5 %factors.1 = (f32[1,1,8,4096]{3,2,1,0:T(8,128)}, f32[1,1,16,64,64]{4,3,2,1,0:T(8,128)}, f32[1,1,10,64,64]{4,3,2,1,0:T(8,128)}) custom-call(f32[16,8,256]{2,1,0:T(8,128)} %get-tuple-element.6.near, f32[8,64,128]{2,1,0:T(8,128)} %get-tuple-element.7.leaf_in, f32[5,64,128]{2,1,0:T(8,128)} %get-tuple-element.8.gram_in), custom_call_target="tpu_custom_call" | custom-call | tf_op jit(solution)/shard_map/factors/pallas_call | solution.py:482

commit v4 on v3

--- a/solution.py
+++ b/solution.py
@@ -122,8 +122,6 @@
     z = ty // 2 + 3 * (1 - (ty * n_tx + tx + n_ty * n_tx - 1) // (n_ty * n_tx))
     near_z, first_z = 1 - z // 4, 1 - (z + 7) // 8
     pairs_ahead = near_z * (4 - z) - first_z
-    columns_ahead = near_z + first_z
-    columns_next = columns_ahead + 1 - near_z
 
     @pl.when(ty == n_ty - 1)
     def _():
@@ -307,11 +305,7 @@
     def own_pairs(first, last, begin):
         loop(last, lambda i: (own_pair(2 * i, 0, begin), own_pair(2 * i + 1, 10, begin)), 1, first)
 
-    def columns(first, last):
-        loop(last, lambda i: (column(2 * i), column(2 * i + 1, 10)), 1, first)
-
     own_pairs(0, pairs_ahead, 0)
-    columns(0, columns_ahead)
     if comm:
         pl.semaphore_wait(barrier, len(peers))
     halo(0).start()
@@ -322,12 +316,7 @@
             halo(j).start()
 
     send_round(0)
-    columns(columns_ahead, columns_next)
-    finish_round(0)
-    send_round(1)
-    columns(columns_next, 2)
-    finish_round(1)
-    send_round(2)
+    loop(2, lambda i: (column(2 * i), column(2 * i + 1, 10)))
     wait_recv(halo(0))
 
     @pl.when(ty < n_ty - 1)
@@ -339,7 +328,11 @@
     done = 4 * pairs_ahead
     loop(2, lambda i: (tx_pair(2 * i), tx_pair(2 * i + 1, 10)))
     reply(0).start()
+    finish_round(0)
+    send_round(1)
     loop(2, lambda i: (ty_pair(2 * i), ty_pair(2 * i + 1, 10)))
+    finish_round(1)
+    send_round(2)
     loop(1, lambda i: (corner_pair(2 * i), corner_pair(2 * i + 1, 10)))
 
     @pl.when(ty < n_ty - 1)

time: 63.7 us -> 53 us (0.83); the launches traced: 63.5 us -> 52 us
  Pallas kernels: 62.7 us -> 51.2 us
    pallas_call x1, Pallas kernels: 56.2 us -> 44.7 us  [on_device(): pl.pallas_call(functools.partial(main_kernel, sizes, comm), out_shape=(ja...]
where the time goes in v4:
time: 53 us; the launch traced here: 52 us
  Pallas kernels  51.2 us (97%)
  between operations  0.82 us (2%)
    pallas_call x1, Pallas kernels, on_device(): pl.pallas_call(functools.partial(main_kernel, sizes, comm), out_shape=(ja...  44.7 us
    pallas_call x1, Pallas kernels, on_device(): pl.pallas_call(factor_kernel, out_shape=(jax.ShapeDtypeStruct((1, 1, 8, B...  6.5 us

profile of v4, /device:TPU:1, one launch (start us, length us, event | category | flops | bytes accessed | tf_op | source)
XLA Modules:
  0.0 52.0 jit_solution(1646898603379453940)
XLA Ops:
  0.6 44.7 %near_and_grams.1 = (f32[16,8,256]{2,1,0:T(8,128)}, f32[8,64,128]{2,1,0:T(8,128)}, f32[5,64,128]{2,1,0:T(8,128)}) custom-call(f32[3,32,128]{2,1,0:T(8,128)} %bitcast.1, f32[1,1,8,4096]{3,2,1,0:T(8,128)} %prb_in.1, s32[1,1,16,27]{3,2,1,0:T(8,128)} %near_in.1, f32[1,1,64,4096]{3,2,1,0:T(8,128)} %leaf_in.1, f32[1,1,16,64,64]{4,3,2,1,0:T(8,128)} %trans_in.1, ...), custom_call_target="tpu_custom_call" | custom-call | tf_op jit(solution)/shard_map/near_and_grams/pallas_call | solution.py:434
  45.4 6.5 %factors.1 = (f32[1,1,8,4096]{3,2,1,0:T(8,128)}, f32[1,1,16,64,64]{4,3,2,1,0:T(8,128)}, f32[1,1,10,64,64]{4,3,2,1,0:T(8,128)}) custom-call(f32[16,8,256]{2,1,0:T(8,128)} %get-tuple-element.6.near, f32[8,64,128]{2,1,0:T(8,128)} %get-tuple-element.7.leaf_in, f32[5,64,128]{2,1,0:T(8,128)} %get-tuple-element.8.gram_in), custom_call_target="tpu_custom_call" | custom-call | tf_op jit(solution)/shard_map/factors/pallas_call | solution.py:475

commit v5 on v4

--- a/solution.py
+++ b/solution.py
@@ -308,6 +308,7 @@
     own_pairs(0, pairs_ahead, 0)
     if comm:
         pl.semaphore_wait(barrier, len(peers))
+    send_round(0)
     halo(0).start()
 
     @pl.when(ty > 0)
@@ -315,8 +316,9 @@
         for j in range(1, 4):
             halo(j).start()
 
-    send_round(0)
     loop(2, lambda i: (column(2 * i), column(2 * i + 1, 10)))
+    finish_round(0)
+    send_round(1)
     wait_recv(halo(0))
 
     @pl.when(ty < n_ty - 1)
@@ -327,12 +329,10 @@
     loop(REMOTE, lambda i: prepare(BOXES + i, False), 4)
     done = 4 * pairs_ahead
     loop(2, lambda i: (tx_pair(2 * i), tx_pair(2 * i + 1, 10)))
-    reply(0).start()
-    finish_round(0)
-    send_round(1)
-    loop(2, lambda i: (ty_pair(2 * i), ty_pair(2 * i + 1, 10)))
     finish_round(1)
     send_round(2)
+    reply(0).start()
+    loop(2, lambda i: (ty_pair(2 * i), ty_pair(2 * i + 1, 10)))
     loop(1, lambda i: (corner_pair(2 * i), corner_pair(2 * i + 1, 10)))
 
     @pl.when(ty < n_ty - 1)
@@ -341,9 +341,6 @@
             reply(j).start()
 
     own_pairs(pairs_ahead, 3, 20)
-    finish_round(2)
-    for i in range(5):
-        gram_out[i] = jnp.concatenate([grams[2 * i], grams[2 * i + 1]], axis=1)
     wait_recv(reply(0))
 
     @pl.when(ty > 0)
@@ -357,6 +354,9 @@
             if start <= i < start + count:
                 value = value + back[at_row + i - start]
         near_out[i] = value
+    finish_round(2)
+    for i in range(5):
+        gram_out[i] = jnp.concatenate([grams[2 * i], grams[2 * i + 1]], axis=1)
     wait_send(halo(0))
     wait_send(reply(0))
 

time: 53 us -> 54.3 us (1.025); the launches traced: 52 us -> 54.1 us
  Pallas kernels: 51.2 us -> 53.3 us
    pallas_call x1, Pallas kernels: 44.7 us -> 46.8 us  [on_device(): pl.pallas_call(functools.partial(main_kernel, sizes, comm), out_shape=(ja...]
where the time goes in v5:
time: 54.3 us; the launch traced here: 54.1 us
  Pallas kernels  53.3 us (98%)
  between operations  0.82 us (2%)
    pallas_call x1, Pallas kernels, on_device(): pl.pallas_call(functools.partial(main_kernel, sizes, comm), out_shape=(ja...  46.8 us
    pallas_call x1, Pallas kernels, on_device(): pl.pallas_call(factor_kernel, out_shape=(jax.ShapeDtypeStruct((1, 1, 8, B...  6.5 us

profile of v5, /device:TPU:1, one launch (start us, length us, event | category | flops | bytes accessed | tf_op | source)
XLA Modules:
  0.0 54.1 jit_solution(17976596461351873193)
XLA Ops:
  0.6 46.8 %near_and_grams.1 = (f32[16,8,256]{2,1,0:T(8,128)}, f32[8,64,128]{2,1,0:T(8,128)}, f32[5,64,128]{2,1,0:T(8,128)}) custom-call(f32[3,32,128]{2,1,0:T(8,128)} %bitcast.1, f32[1,1,8,4096]{3,2,1,0:T(8,128)} %prb_in.1, s32[1,1,16,27]{3,2,1,0:T(8,128)} %near_in.1, f32[1,1,64,4096]{3,2,1,0:T(8,128)} %leaf_in.1, f32[1,1,16,64,64]{4,3,2,1,0:T(8,128)} %trans_in.1, ...), custom_call_target="tpu_custom_call" | custom-call | tf_op jit(solution)/shard_map/near_and_grams/pallas_call | solution.py:434
  47.5 6.5 %factors.1 = (f32[1,1,8,4096]{3,2,1,0:T(8,128)}, f32[1,1,16,64,64]{4,3,2,1,0:T(8,128)}, f32[1,1,10,64,64]{4,3,2,1,0:T(8,128)}) custom-call(f32[16,8,256]{2,1,0:T(8,128)} %get-tuple-element.6.near, f32[8,64,128]{2,1,0:T(8,128)} %get-tuple-element.7.leaf_in, f32[5,64,128]{2,1,0:T(8,128)} %get-tuple-element.8.gram_in), custom_call_target="tpu_custom_call" | custom-call | tf_op jit(solution)/shard_map/factors/pallas_call | solution.py:475
